TPU v7x, 1024 devices: a whole 8x8x8 slice. The times are simulated.
1024 devices in a mesh: row: 64 (over y, x_hi, core), col: 16 (over z, x_lo).
Axes of the slice: x: 8 (x_hi: 4, x_lo: 2; x = x_hi * 2 + x_lo), y: 8, z: 8, core: 2. Of those that a mesh axis runs over, the one named last changes fastest.
Arguments:
- a_blocks: bfloat16 [16, 64, 128, 128], P('col', 'row'), may hold values from -6 to 6
- a_rows: int32 [16, 64], P('col', 'row'), may hold values from 0 to 1, as said below
- b_blocks: bfloat16 [2, 64, 64, 128, 128], P(None, 'row', 'col'), may hold values from -0.25 to 0.25
- b_cols: int32 [2, 64, 64], P(None, 'row', 'col'), may hold values from 0 to 15
- owner: int32 [16, 64, 16], P('col', 'row'), may hold values from 0 to 15, each once within a row
Outputs:
- delivered: bfloat16 [2, 16, 64, 16, 128, 128], P(None, 'col', 'row')
Inputs may be any that keep to these rules, and one draw needn't show every extreme that they name: `a_rows`: A value below 1 is the block row of the panel's one occupied block; 1 marks a panel without a block. `owner`: each panel pair's last dimension is a permutation of 0 to 15.
All inputs are finite; a program needn't handle non-finite values.
Results may differ from a plain program's by a relative error of at most 0.001.
Values may be sent and summed in bfloat16 or wider, within the bound.
No kernel may reach another device: no remote copies, remote signals or barrier semaphores. Data moves between devices by JAX's collectives and lax.ppermute only.
A program may use at most 64 MiB of HBM per device.

v0:
```python
import jax
import jax.numpy as jnp
from jax import lax
from jax.sharding import PartitionSpec as P

LB = 16
BR = 1


def for_sending(value):

    def short(part):
        return part.astype(jnp.bfloat16) if part.dtype == jnp.float32 else part

    return jax.tree.map(short, value)


def from_behind(block, axis, distance):
    devices = range(lax.axis_size(axis))
    route = [((i - distance) % len(devices), i) for i in devices]
    return lax.ppermute(block, axis, route)


def fold_batch(totals, a_stack, row_list, b_stack, col_list):
    slot_ids = jnp.arange(totals.shape[1], dtype=jnp.int32)
    occupied = row_list < BR
    products = jnp.einsum("kij,okjl->okil", a_stack, b_stack, preferred_element_type=jnp.float32)
    target_slot = row_list[None, :] * LB + col_list
    selector = jnp.logical_and(
        target_slot[:, :, None] == slot_ids[None, None, :], occupied[None, :, None]
    ).astype(jnp.float32)
    return totals + jnp.einsum(
        "oks,okil->osil", selector, products, precision=lax.Precision.HIGHEST
    )


def shards(a_blocks, a_rows, b_blocks, b_cols, owner):
    block_edge = a_blocks.shape[2]
    slot_count = owner.shape[2]
    group_size = b_blocks.shape[2]
    totals = jnp.zeros((2, slot_count, block_edge, block_edge), jnp.float32)

    def one_round(current, a_pair, b_pair, final):
        block_list = []
        row_items = []
        for within in range(group_size):
            block_list.append(a_pair[0][0, 0])
            row_items.append(a_pair[1][0, 0])
            if not (final and within == group_size - 1):
                a_pair = jax.tree.map(
                    lambda part, own: part.astype(own.dtype),
                    from_behind(for_sending(a_pair), "row", 1),
                    a_pair,
                )
        a_stack = jnp.stack(block_list)
        row_list = jnp.stack(row_items).astype(jnp.int32)
        current = fold_batch(current, a_stack, row_list, b_pair[0][:, 0], b_pair[1][:, 0])
        return (current, a_pair)

    def step_round(step_index, carry):
        current, a_pair, b_pair = carry
        current, a_pair = one_round(current, a_pair, b_pair, False)
        b_pair = jax.tree.map(
            lambda part, own: part.astype(own.dtype),
            from_behind(for_sending(b_pair), "col", -1),
            b_pair,
        )
        return (current, a_pair, b_pair)

    carry = lax.fori_loop(
        0, lax.axis_size("col") - 1, step_round, (totals, (a_blocks, a_rows), (b_blocks, b_cols))
    )
    totals, last_a = one_round(carry[0], carry[1], carry[2], True)
    send_order = jnp.argsort(owner[0, 0])
    outgoing = totals.astype(jnp.bfloat16)[:, send_order]
    arrived = lax.all_to_all(outgoing, "col", split_axis=1, concat_axis=1, tiled=True)
    return arrived.reshape(2, 1, 1, slot_count, block_edge, block_edge)


def solution(mesh):
    in_specs = (
        P("col", "row", None, None),
        P("col", "row"),
        P(None, "row", "col", None, None),
        P(None, "row", "col"),
        P("col", "row", None),
    )
    out_specs = P(None, "col", "row", None, None, None)
    return jax.shard_map(shards, mesh=mesh, in_specs=in_specs, out_specs=out_specs, check_vma=False)
```

profile of v0, /device:TPU:64, one launch (start us, length us, event | category | flops | bytes accessed | tf_op | source)
XLA Modules:
  0.0 1021.5 jit_solution(4919324879601893811)
XLA Ops:
  3.1 929.8 %while.19 = (s32[]{:T(128)}, f32[2,16,128,128]{3,1,2,0:T(8,128)S(1)}, bf16[1,1,128,128]{3,2,1,0:T(8,128)(2,1)S(1)}, s32[1,1]{1,0:T(1,128)}, bf16[2,1,4,128,128]{...) while((s32[]{:T(128)}, f32[2,16,128,128]{3,1,2,0:T(8,128)S(1)}, ...), condition=%wide.region_1.0_spmd.clone, body=%wide.region_0.0_spmd.clone.sunk | while | flops 60293404 | bytes 7734183 | solution.py:70
  10.1 18.2 %collective-permute-start.8 = (bf16[2,1,4,128,128]{4,3,2,1,0:T(8,128)(2,1)S(1)}, bf16[2,1,4,128,128]{4,3,2,1,0:T(8,128)(2,1)S(1)}, u32[]{:S(2)}, u32[]{:S(2)}) collective-permute-start(bf16[2,1,4,128,128]{4,3,2,1,0:T(8,128)(2,1)S(1)} %copy.41), channel_id=1, source_target_pairs={{1,0},{2,1},{3,2},{4,3},{5,4},{6,5},{7,6},{8,7},{9,8},{10,9},{11,1... | collective-permute-start | bytes 786440 | tf_op jit(solution)/shard_map/while/body/eval_jaxpr/ppermute | solution.py:21
  53.2 7.8 collective-permute-done.1
  92.4 7.8 collective-permute-done.4
  113.4 7.6 collective-permute-done.1
  152.5 7.8 collective-permute-done.4
  173.6 7.6 collective-permute-done.1
  212.6 7.8 collective-permute-done.4
  233.7 7.6 collective-permute-done.1
  272.2 7.9 collective-permute-done.4
  293.4 7.5 collective-permute-done.1
  331.8 7.9 collective-permute-done.4
  353.0 7.5 collective-permute-done.1
  391.4 7.9 collective-permute-done.4
  412.6 7.5 collective-permute-done.1
  451.0 7.9 collective-permute-done.4
  504.2 17.1 %collective-permute-start.8 = (bf16[2,1,4,128,128]{4,3,2,1,0:T(8,128)(2,1)S(1)}, bf16[2,1,4,128,128]{4,3,2,1,0:T(8,128)(2,1)S(1)}, u32[]{:S(2)}, u32[]{:S(2)}) collective-permute-start(bf16[2,1,4,128,128]{4,3,2,1,0:T(8,128)(2,1)S(1)} %copy.41), channel_id=1, source_target_pairs={{1,0},{2,1},{3,2},{4,3},{5,4},{6,5},{7,6},{8,7},{9,8},{10,9},{11,1... | collective-permute-start | bytes 786440 | tf_op jit(solution)/shard_map/while/body/eval_jaxpr/ppermute | solution.py:21
  525.4 7.8 collective-permute-done.4
  546.4 7.6 collective-permute-done.1
  585.5 7.8 collective-permute-done.4
  606.5 7.6 collective-permute-done.1
  645.6 7.8 collective-permute-done.4
  666.6 7.6 collective-permute-done.1
  705.7 7.8 collective-permute-done.4
  726.7 7.6 collective-permute-done.1
  765.3 7.9 collective-permute-done.4
  786.4 7.5 collective-permute-done.1
  824.9 7.9 collective-permute-done.4
  846.0 7.5 collective-permute-done.1
  884.5 7.9 collective-permute-done.4
  964.2 7.5 collective-permute-done.14
  984.0 36.4 %all_to_all.5 = bf16[2,16,128,128]{3,2,0,1:T(8,128)(2,1)S(1)} all-to-all(bf16[2,16,128,128]{3,2,0,1:T(8,128)(2,1)S(1)} %bitcast.84), channel_id=1, replica_groups=mesh['row'=64,'col'=16] {'col'}, dimensions={1} | all-to-all | bytes 2097152 | tf_op jit(solution)/shard_map/all_to_all | solution.py:76
  (406 shorter events, 720.9 us)
Async XLA Ops:
  5.9 45.3 %collective-permute-start = (bf16[1,1,128,128]{3,2,1,0:T(8,128)(2,1)S(1)}, bf16[1,1,128,128]{3,2,1,0:T(8,128)(2,1)S(1)}, u32[]{:S(2)}, u32[]{:S(2)}) collective-permute-start(bf16[1,1,128,128]{3,2,1,0:T(8,128)(2,1)S(1)} %get-tuple-element.148), channel_id=1, source_target_pairs={{1008,0},{0,16},{16,32},{32,48},{48,64},{64,80},{80,96},{96,112},{... | collective-permute-start | bytes 98312 | tf_op jit(solution)/shard_map/while/body/eval_jaxpr/ppermute | solution.py:21
  10.1 69.9 %collective-permute-start.8 = (bf16[2,1,4,128,128]{4,3,2,1,0:T(8,128)(2,1)S(1)}, bf16[2,1,4,128,128]{4,3,2,1,0:T(8,128)(2,1)S(1)}, u32[]{:S(2)}, u32[]{:S(2)}) collective-permute-start(bf16[2,1,4,128,128]{4,3,2,1,0:T(8,128)(2,1)S(1)} %copy.41), channel_id=1, source_target_pairs={{1,0},{2,1},{3,2},{4,3},{5,4},{6,5},{7,6},{8,7},{9,8},{10,9},{11,1... | collective-permute-start | bytes 786440 | tf_op jit(solution)/shard_map/while/body/eval_jaxpr/ppermute | solution.py:21
  28.4 46.5 %collective-permute-start.9 = (s32[2,1,4]{2,0,1:T(2,128)S(1)}, s32[2,1,4]{2,0,1:T(2,128)S(1)}, u32[]{:S(2)}, u32[]{:S(2)}) collective-permute-start(s32[2,1,4]{2,0,1:T(2,128)S(1)} %copy.42), channel_id=1, source_target_pairs={{1,0},{2,1},{3,2},{4,3},{5,4},{6,5},{7,6},{8,7},{9,8},{10,9},{11,1... | collective-permute-start | bytes 104 | tf_op jit(solution)/shard_map/while/body/eval_jaxpr/ppermute | solution.py:21
  85.5 54.7 %collective-permute-start.8 = (bf16[2,1,4,128,128]{4,3,2,1,0:T(8,128)(2,1)S(1)}, bf16[2,1,4,128,128]{4,3,2,1,0:T(8,128)(2,1)S(1)}, u32[]{:S(2)}, u32[]{:S(2)}) collective-permute-start(bf16[2,1,4,128,128]{4,3,2,1,0:T(8,128)(2,1)S(1)} %copy.41), channel_id=1, source_target_pairs={{1,0},{2,1},{3,2},{4,3},{5,4},{6,5},{7,6},{8,7},{9,8},{10,9},{11,1... | collective-permute-start | bytes 786440 | tf_op jit(solution)/shard_map/while/body/eval_jaxpr/ppermute | solution.py:21
  88.5 46.6 %collective-permute-start.9 = (s32[2,1,4]{2,0,1:T(2,128)S(1)}, s32[2,1,4]{2,0,1:T(2,128)S(1)}, u32[]{:S(2)}, u32[]{:S(2)}) collective-permute-start(s32[2,1,4]{2,0,1:T(2,128)S(1)} %copy.42), channel_id=1, source_target_pairs={{1,0},{2,1},{3,2},{4,3},{5,4},{6,5},{7,6},{8,7},{9,8},{10,9},{11,1... | collective-permute-start | bytes 104 | tf_op jit(solution)/shard_map/while/body/eval_jaxpr/ppermute | solution.py:21
  145.6 54.7 %collective-permute-start.8 = (bf16[2,1,4,128,128]{4,3,2,1,0:T(8,128)(2,1)S(1)}, bf16[2,1,4,128,128]{4,3,2,1,0:T(8,128)(2,1)S(1)}, u32[]{:S(2)}, u32[]{:S(2)}) collective-permute-start(bf16[2,1,4,128,128]{4,3,2,1,0:T(8,128)(2,1)S(1)} %copy.41), channel_id=1, source_target_pairs={{1,0},{2,1},{3,2},{4,3},{5,4},{6,5},{7,6},{8,7},{9,8},{10,9},{11,1... | collective-permute-start | bytes 786440 | tf_op jit(solution)/shard_map/while/body/eval_jaxpr/ppermute | solution.py:21
  148.6 46.6 %collective-permute-start.9 = (s32[2,1,4]{2,0,1:T(2,128)S(1)}, s32[2,1,4]{2,0,1:T(2,128)S(1)}, u32[]{:S(2)}, u32[]{:S(2)}) collective-permute-start(s32[2,1,4]{2,0,1:T(2,128)S(1)} %copy.42), channel_id=1, source_target_pairs={{1,0},{2,1},{3,2},{4,3},{5,4},{6,5},{7,6},{8,7},{9,8},{10,9},{11,1... | collective-permute-start | bytes 104 | tf_op jit(solution)/shard_map/while/body/eval_jaxpr/ppermute | solution.py:21
  205.8 54.7 %collective-permute-start.8 = (bf16[2,1,4,128,128]{4,3,2,1,0:T(8,128)(2,1)S(1)}, bf16[2,1,4,128,128]{4,3,2,1,0:T(8,128)(2,1)S(1)}, u32[]{:S(2)}, u32[]{:S(2)}) collective-permute-start(bf16[2,1,4,128,128]{4,3,2,1,0:T(8,128)(2,1)S(1)} %copy.41), channel_id=1, source_target_pairs={{1,0},{2,1},{3,2},{4,3},{5,4},{6,5},{7,6},{8,7},{9,8},{10,9},{11,1... | collective-permute-start | bytes 786440 | tf_op jit(solution)/shard_map/while/body/eval_jaxpr/ppermute | solution.py:21
  208.7 46.6 %collective-permute-start.9 = (s32[2,1,4]{2,0,1:T(2,128)S(1)}, s32[2,1,4]{2,0,1:T(2,128)S(1)}, u32[]{:S(2)}, u32[]{:S(2)}) collective-permute-start(s32[2,1,4]{2,0,1:T(2,128)S(1)} %copy.42), channel_id=1, source_target_pairs={{1,0},{2,1},{3,2},{4,3},{5,4},{6,5},{7,6},{8,7},{9,8},{10,9},{11,1... | collective-permute-start | bytes 104 | tf_op jit(solution)/shard_map/while/body/eval_jaxpr/ppermute | solution.py:21
  265.9 54.2 %collective-permute-start.8 = (bf16[2,1,4,128,128]{4,3,2,1,0:T(8,128)(2,1)S(1)}, bf16[2,1,4,128,128]{4,3,2,1,0:T(8,128)(2,1)S(1)}, u32[]{:S(2)}, u32[]{:S(2)}) collective-permute-start(bf16[2,1,4,128,128]{4,3,2,1,0:T(8,128)(2,1)S(1)} %copy.41), channel_id=1, source_target_pairs={{1,0},{2,1},{3,2},{4,3},{5,4},{6,5},{7,6},{8,7},{9,8},{10,9},{11,1... | collective-permute-start | bytes 786440 | tf_op jit(solution)/shard_map/while/body/eval_jaxpr/ppermute | solution.py:21
  267.8 47.0 %collective-permute-start.9 = (s32[2,1,4]{2,0,1:T(2,128)S(1)}, s32[2,1,4]{2,0,1:T(2,128)S(1)}, u32[]{:S(2)}, u32[]{:S(2)}) collective-permute-start(s32[2,1,4]{2,0,1:T(2,128)S(1)} %copy.42), channel_id=1, source_target_pairs={{1,0},{2,1},{3,2},{4,3},{5,4},{6,5},{7,6},{8,7},{9,8},{10,9},{11,1... | collective-permute-start | bytes 104 | tf_op jit(solution)/shard_map/while/body/eval_jaxpr/ppermute | solution.py:21
  325.5 54.2 %collective-permute-start.8 = (bf16[2,1,4,128,128]{4,3,2,1,0:T(8,128)(2,1)S(1)}, bf16[2,1,4,128,128]{4,3,2,1,0:T(8,128)(2,1)S(1)}, u32[]{:S(2)}, u32[]{:S(2)}) collective-permute-start(bf16[2,1,4,128,128]{4,3,2,1,0:T(8,128)(2,1)S(1)} %copy.41), channel_id=1, source_target_pairs={{1,0},{2,1},{3,2},{4,3},{5,4},{6,5},{7,6},{8,7},{9,8},{10,9},{11,1... | collective-permute-start | bytes 786440 | tf_op jit(solution)/shard_map/while/body/eval_jaxpr/ppermute | solution.py:21
  327.4 47.0 %collective-permute-start.9 = (s32[2,1,4]{2,0,1:T(2,128)S(1)}, s32[2,1,4]{2,0,1:T(2,128)S(1)}, u32[]{:S(2)}, u32[]{:S(2)}) collective-permute-start(s32[2,1,4]{2,0,1:T(2,128)S(1)} %copy.42), channel_id=1, source_target_pairs={{1,0},{2,1},{3,2},{4,3},{5,4},{6,5},{7,6},{8,7},{9,8},{10,9},{11,1... | collective-permute-start | bytes 104 | tf_op jit(solution)/shard_map/while/body/eval_jaxpr/ppermute | solution.py:21
  385.1 54.2 %collective-permute-start.8 = (bf16[2,1,4,128,128]{4,3,2,1,0:T(8,128)(2,1)S(1)}, bf16[2,1,4,128,128]{4,3,2,1,0:T(8,128)(2,1)S(1)}, u32[]{:S(2)}, u32[]{:S(2)}) collective-permute-start(bf16[2,1,4,128,128]{4,3,2,1,0:T(8,128)(2,1)S(1)} %copy.41), channel_id=1, source_target_pairs={{1,0},{2,1},{3,2},{4,3},{5,4},{6,5},{7,6},{8,7},{9,8},{10,9},{11,1... | collective-permute-start | bytes 786440 | tf_op jit(solution)/shard_map/while/body/eval_jaxpr/ppermute | solution.py:21
  387.0 47.0 %collective-permute-start.9 = (s32[2,1,4]{2,0,1:T(2,128)S(1)}, s32[2,1,4]{2,0,1:T(2,128)S(1)}, u32[]{:S(2)}, u32[]{:S(2)}) collective-permute-start(s32[2,1,4]{2,0,1:T(2,128)S(1)} %copy.42), channel_id=1, source_target_pairs={{1,0},{2,1},{3,2},{4,3},{5,4},{6,5},{7,6},{8,7},{9,8},{10,9},{11,1... | collective-permute-start | bytes 104 | tf_op jit(solution)/shard_map/while/body/eval_jaxpr/ppermute | solution.py:21
  444.6 54.2 %collective-permute-start.8 = (bf16[2,1,4,128,128]{4,3,2,1,0:T(8,128)(2,1)S(1)}, bf16[2,1,4,128,128]{4,3,2,1,0:T(8,128)(2,1)S(1)}, u32[]{:S(2)}, u32[]{:S(2)}) collective-permute-start(bf16[2,1,4,128,128]{4,3,2,1,0:T(8,128)(2,1)S(1)} %copy.41), channel_id=1, source_target_pairs={{1,0},{2,1},{3,2},{4,3},{5,4},{6,5},{7,6},{8,7},{9,8},{10,9},{11,1... | collective-permute-start | bytes 786440 | tf_op jit(solution)/shard_map/while/body/eval_jaxpr/ppermute | solution.py:21
  446.6 47.0 %collective-permute-start.9 = (s32[2,1,4]{2,0,1:T(2,128)S(1)}, s32[2,1,4]{2,0,1:T(2,128)S(1)}, u32[]{:S(2)}, u32[]{:S(2)}) collective-permute-start(s32[2,1,4]{2,0,1:T(2,128)S(1)} %copy.42), channel_id=1, source_target_pairs={{1,0},{2,1},{3,2},{4,3},{5,4},{6,5},{7,6},{8,7},{9,8},{10,9},{11,1... | collective-permute-start | bytes 104 | tf_op jit(solution)/shard_map/while/body/eval_jaxpr/ppermute | solution.py:21
  502.3 42.1 %collective-permute-start = (bf16[1,1,128,128]{3,2,1,0:T(8,128)(2,1)S(1)}, bf16[1,1,128,128]{3,2,1,0:T(8,128)(2,1)S(1)}, u32[]{:S(2)}, u32[]{:S(2)}) collective-permute-start(bf16[1,1,128,128]{3,2,1,0:T(8,128)(2,1)S(1)} %get-tuple-element.148), channel_id=1, source_target_pairs={{1008,0},{0,16},{16,32},{32,48},{48,64},{64,80},{80,96},{96,112},{... | collective-permute-start | bytes 98312 | tf_op jit(solution)/shard_map/while/body/eval_jaxpr/ppermute | solution.py:21
  504.2 68.9 %collective-permute-start.8 = (bf16[2,1,4,128,128]{4,3,2,1,0:T(8,128)(2,1)S(1)}, bf16[2,1,4,128,128]{4,3,2,1,0:T(8,128)(2,1)S(1)}, u32[]{:S(2)}, u32[]{:S(2)}) collective-permute-start(bf16[2,1,4,128,128]{4,3,2,1,0:T(8,128)(2,1)S(1)} %copy.41), channel_id=1, source_target_pairs={{1,0},{2,1},{3,2},{4,3},{5,4},{6,5},{7,6},{8,7},{9,8},{10,9},{11,1... | collective-permute-start | bytes 786440 | tf_op jit(solution)/shard_map/while/body/eval_jaxpr/ppermute | solution.py:21
  521.4 46.6 %collective-permute-start.9 = (s32[2,1,4]{2,0,1:T(2,128)S(1)}, s32[2,1,4]{2,0,1:T(2,128)S(1)}, u32[]{:S(2)}, u32[]{:S(2)}) collective-permute-start(s32[2,1,4]{2,0,1:T(2,128)S(1)} %copy.42), channel_id=1, source_target_pairs={{1,0},{2,1},{3,2},{4,3},{5,4},{6,5},{7,6},{8,7},{9,8},{10,9},{11,1... | collective-permute-start | bytes 104 | tf_op jit(solution)/shard_map/while/body/eval_jaxpr/ppermute | solution.py:21
  578.6 54.7 %collective-permute-start.8 = (bf16[2,1,4,128,128]{4,3,2,1,0:T(8,128)(2,1)S(1)}, bf16[2,1,4,128,128]{4,3,2,1,0:T(8,128)(2,1)S(1)}, u32[]{:S(2)}, u32[]{:S(2)}) collective-permute-start(bf16[2,1,4,128,128]{4,3,2,1,0:T(8,128)(2,1)S(1)} %copy.41), channel_id=1, source_target_pairs={{1,0},{2,1},{3,2},{4,3},{5,4},{6,5},{7,6},{8,7},{9,8},{10,9},{11,1... | collective-permute-start | bytes 786440 | tf_op jit(solution)/shard_map/while/body/eval_jaxpr/ppermute | solution.py:21
  581.5 46.6 %collective-permute-start.9 = (s32[2,1,4]{2,0,1:T(2,128)S(1)}, s32[2,1,4]{2,0,1:T(2,128)S(1)}, u32[]{:S(2)}, u32[]{:S(2)}) collective-permute-start(s32[2,1,4]{2,0,1:T(2,128)S(1)} %copy.42), channel_id=1, source_target_pairs={{1,0},{2,1},{3,2},{4,3},{5,4},{6,5},{7,6},{8,7},{9,8},{10,9},{11,1... | collective-permute-start | bytes 104 | tf_op jit(solution)/shard_map/while/body/eval_jaxpr/ppermute | solution.py:21
  638.7 54.7 %collective-permute-start.8 = (bf16[2,1,4,128,128]{4,3,2,1,0:T(8,128)(2,1)S(1)}, bf16[2,1,4,128,128]{4,3,2,1,0:T(8,128)(2,1)S(1)}, u32[]{:S(2)}, u32[]{:S(2)}) collective-permute-start(bf16[2,1,4,128,128]{4,3,2,1,0:T(8,128)(2,1)S(1)} %copy.41), channel_id=1, source_target_pairs={{1,0},{2,1},{3,2},{4,3},{5,4},{6,5},{7,6},{8,7},{9,8},{10,9},{11,1... | collective-permute-start | bytes 786440 | tf_op jit(solution)/shard_map/while/body/eval_jaxpr/ppermute | solution.py:21
  641.6 46.6 %collective-permute-start.9 = (s32[2,1,4]{2,0,1:T(2,128)S(1)}, s32[2,1,4]{2,0,1:T(2,128)S(1)}, u32[]{:S(2)}, u32[]{:S(2)}) collective-permute-start(s32[2,1,4]{2,0,1:T(2,128)S(1)} %copy.42), channel_id=1, source_target_pairs={{1,0},{2,1},{3,2},{4,3},{5,4},{6,5},{7,6},{8,7},{9,8},{10,9},{11,1... | collective-permute-start | bytes 104 | tf_op jit(solution)/shard_map/while/body/eval_jaxpr/ppermute | solution.py:21
  698.8 54.7 %collective-permute-start.8 = (bf16[2,1,4,128,128]{4,3,2,1,0:T(8,128)(2,1)S(1)}, bf16[2,1,4,128,128]{4,3,2,1,0:T(8,128)(2,1)S(1)}, u32[]{:S(2)}, u32[]{:S(2)}) collective-permute-start(bf16[2,1,4,128,128]{4,3,2,1,0:T(8,128)(2,1)S(1)} %copy.41), channel_id=1, source_target_pairs={{1,0},{2,1},{3,2},{4,3},{5,4},{6,5},{7,6},{8,7},{9,8},{10,9},{11,1... | collective-permute-start | bytes 786440 | tf_op jit(solution)/shard_map/while/body/eval_jaxpr/ppermute | solution.py:21
  701.7 46.6 %collective-permute-start.9 = (s32[2,1,4]{2,0,1:T(2,128)S(1)}, s32[2,1,4]{2,0,1:T(2,128)S(1)}, u32[]{:S(2)}, u32[]{:S(2)}) collective-permute-start(s32[2,1,4]{2,0,1:T(2,128)S(1)} %copy.42), channel_id=1, source_target_pairs={{1,0},{2,1},{3,2},{4,3},{5,4},{6,5},{7,6},{8,7},{9,8},{10,9},{11,1... | collective-permute-start | bytes 104 | tf_op jit(solution)/shard_map/while/body/eval_jaxpr/ppermute | solution.py:21
  758.9 54.2 %collective-permute-start.8 = (bf16[2,1,4,128,128]{4,3,2,1,0:T(8,128)(2,1)S(1)}, bf16[2,1,4,128,128]{4,3,2,1,0:T(8,128)(2,1)S(1)}, u32[]{:S(2)}, u32[]{:S(2)}) collective-permute-start(bf16[2,1,4,128,128]{4,3,2,1,0:T(8,128)(2,1)S(1)} %copy.41), channel_id=1, source_target_pairs={{1,0},{2,1},{3,2},{4,3},{5,4},{6,5},{7,6},{8,7},{9,8},{10,9},{11,1... | collective-permute-start | bytes 786440 | tf_op jit(solution)/shard_map/while/body/eval_jaxpr/ppermute | solution.py:21
  760.8 47.0 %collective-permute-start.9 = (s32[2,1,4]{2,0,1:T(2,128)S(1)}, s32[2,1,4]{2,0,1:T(2,128)S(1)}, u32[]{:S(2)}, u32[]{:S(2)}) collective-permute-start(s32[2,1,4]{2,0,1:T(2,128)S(1)} %copy.42), channel_id=1, source_target_pairs={{1,0},{2,1},{3,2},{4,3},{5,4},{6,5},{7,6},{8,7},{9,8},{10,9},{11,1... | collective-permute-start | bytes 104 | tf_op jit(solution)/shard_map/while/body/eval_jaxpr/ppermute | solution.py:21
  818.5 54.2 %collective-permute-start.8 = (bf16[2,1,4,128,128]{4,3,2,1,0:T(8,128)(2,1)S(1)}, bf16[2,1,4,128,128]{4,3,2,1,0:T(8,128)(2,1)S(1)}, u32[]{:S(2)}, u32[]{:S(2)}) collective-permute-start(bf16[2,1,4,128,128]{4,3,2,1,0:T(8,128)(2,1)S(1)} %copy.41), channel_id=1, source_target_pairs={{1,0},{2,1},{3,2},{4,3},{5,4},{6,5},{7,6},{8,7},{9,8},{10,9},{11,1... | collective-permute-start | bytes 786440 | tf_op jit(solution)/shard_map/while/body/eval_jaxpr/ppermute | solution.py:21
  820.4 47.0 %collective-permute-start.9 = (s32[2,1,4]{2,0,1:T(2,128)S(1)}, s32[2,1,4]{2,0,1:T(2,128)S(1)}, u32[]{:S(2)}, u32[]{:S(2)}) collective-permute-start(s32[2,1,4]{2,0,1:T(2,128)S(1)} %copy.42), channel_id=1, source_target_pairs={{1,0},{2,1},{3,2},{4,3},{5,4},{6,5},{7,6},{8,7},{9,8},{10,9},{11,1... | collective-permute-start | bytes 104 | tf_op jit(solution)/shard_map/while/body/eval_jaxpr/ppermute | solution.py:21
  878.1 54.2 %collective-permute-start.8 = (bf16[2,1,4,128,128]{4,3,2,1,0:T(8,128)(2,1)S(1)}, bf16[2,1,4,128,128]{4,3,2,1,0:T(8,128)(2,1)S(1)}, u32[]{:S(2)}, u32[]{:S(2)}) collective-permute-start(bf16[2,1,4,128,128]{4,3,2,1,0:T(8,128)(2,1)S(1)} %copy.41), channel_id=1, source_target_pairs={{1,0},{2,1},{3,2},{4,3},{5,4},{6,5},{7,6},{8,7},{9,8},{10,9},{11,1... | collective-permute-start | bytes 786440 | tf_op jit(solution)/shard_map/while/body/eval_jaxpr/ppermute | solution.py:21
  880.0 47.0 %collective-permute-start.9 = (s32[2,1,4]{2,0,1:T(2,128)S(1)}, s32[2,1,4]{2,0,1:T(2,128)S(1)}, u32[]{:S(2)}, u32[]{:S(2)}) collective-permute-start(s32[2,1,4]{2,0,1:T(2,128)S(1)} %copy.42), channel_id=1, source_target_pairs={{1,0},{2,1},{3,2},{4,3},{5,4},{6,5},{7,6},{8,7},{9,8},{10,9},{11,1... | collective-permute-start | bytes 104 | tf_op jit(solution)/shard_map/while/body/eval_jaxpr/ppermute | solution.py:21
  (125 other events, 2436.1 us)
where the time goes:
time: 1030 us; the launch traced here: 1020 us
  waiting for transfers between devices  537 us (52%)
  starting transfers between devices  359 us (35%)
  matrix products  39.6 us (4%)
  blocking collectives  36.4 us (4%)
  other arithmetic  31.8 us (3%)
  loops' own time  11.9 us (1%)
    ppermute x156, waiting for transfers between devices, from_behind(): return lax.ppermute(block, axis, route)  537 us
    ppermute x156, starting transfers between devices, from_behind(): return lax.ppermute(block, axis, route)  359 us
    all_to_all x1, blocking collectives, shards(): lax.all_to_all(outgoing, 'col', split_axis=1, concat_axis=1, tiled=True)  36.4 us
    dot_general x16, matrix products, fold_batch(): jnp.einsum('oks,okil->osil', selector, products, precision=lax.Precision....  36.1 us
    lt x16, other arithmetic, fold_batch(): occupied = row_list < BR  30.4 us
  transfers between devices with their start and end apart: 156, of which 80 were waited for; matrix products, arithmetic and copies ran while one was open for 7% of the time, Pallas kernels for 0%

commit v1 on v0

v1 whole, which is shorter than its diff:
```python
import jax
import jax.numpy as jnp
from jax import lax
from jax.experimental import pallas as pl
from jax.experimental.pallas import tpu as pltpu
from jax.sharding import Mesh
from jax.sharding import PartitionSpec as P

BR = 1
CORES = 2
X_LO = 2
X_HI = 4
ROW = ("y", "x_hi", "core")
COL = ("z", "x_lo")


def multiply(place_ref, owner_ref, own_ref, partner_ref, *refs):
    b_refs, (out_ref, total, label_rows, labels, arrived) = refs[:-5], refs[-5:]
    cores, half = CORES, own_ref.shape[0]
    panels = cores * half
    edge = own_ref.shape[1]
    sides = [side for ref in b_refs for side in ([ref] if len(ref.shape) == 2 else [ref.at[i] for i in range(ref.shape[0])])]
    planes = len(sides) // X_LO
    group = panels // len(sides)
    for n, side_ref in enumerate(sides):
        row = side_ref[pl.ds(2 * group * edge, 16), :].astype(jnp.float32)[:8]
        label_rows[pl.ds(8 * n, 8), :] = row.astype(jnp.int32)
    copy = pltpu.make_async_copy(label_rows, labels, arrived)
    copy.start()
    total[...] = jnp.zeros_like(total)
    copy.wait()
    base, here, core = place_ref[0], place_ref[1], place_ref[2]

    for n, side_ref in enumerate(sides):
        plane = lax.rem(here + planes - n // X_LO, planes)
        for j in range(group):
            m = (plane * X_LO + n % X_LO) * group + j
            q = lax.rem(base + panels - m, panels)
            mine = lax.rem(q, cores) == core
            a = jnp.where(mine, own_ref[q // cores], partner_ref[q // cores])
            for o in range(2):
                target = owner_ref[labels[8 * n, o * group + j]]
                b = side_ref[pl.ds((o * group + j) * edge, edge), :]
                total[target, o] += jnp.dot(a, b, preferred_element_type=jnp.float32)
    out_ref[...] = total[...].astype(out_ref.dtype)


def block_products(place, owner, a_own, a_partner, b_pieces):
    slots, edge = owner.shape[0], a_own.shape[-1]
    smem = pl.BlockSpec(memory_space=pltpu.SMEM)
    vmem = pl.BlockSpec(memory_space=pltpu.VMEM)
    label_shape = (8 * lax.axis_size(COL), edge)
    return pl.pallas_call(
        multiply,
        out_shape=jax.ShapeDtypeStruct((slots, 2, edge, edge), jnp.bfloat16),
        in_specs=[smem, smem] + [vmem] * (2 + len(b_pieces)),
        out_specs=vmem,
        scratch_shapes=[
            pltpu.VMEM((slots, 2, edge, edge), jnp.float32),
            pltpu.VMEM(label_shape, jnp.int32),
            pltpu.SMEM(label_shape, jnp.int32),
            pltpu.SemaphoreType.DMA,
        ],
        compiler_params=pltpu.CompilerParams(vmem_limit_bytes=24 * 1024 * 1024),
    )(place, owner, a_own, a_partner, *b_pieces)


def around(piece, axis):
    n = lax.axis_size(axis)
    up = [(i, (i + 1) % n) for i in range(n)]
    down = [(i, (i - 1) % n) for i in range(n)]
    found = [piece] + [None] * (n - 1)
    for t in range(1, (n - 1) // 2 + 1):
        found[t] = lax.ppermute(found[t - 1], axis, up)
        found[n - t] = lax.ppermute(found[(n - t + 1) % n], axis, down)
    far = n // 2
    found[far : far + 1] = [
        lax.ppermute(found[far - 1][0], axis, up),
        lax.ppermute(found[(far + 1) % n][1], axis, down),
    ]
    return found


def shards(a_blocks, a_rows, b_blocks, b_cols, owner):
    edge = a_blocks.shape[-1]
    panels = lax.axis_size(ROW)
    group = b_blocks.shape[2]
    a_own = jnp.where(a_rows[0, 0] < BR, a_blocks[0, 0], jnp.zeros_like(a_blocks[0, 0]))
    labels = jnp.pad(b_cols.reshape(1, -1).astype(jnp.bfloat16), ((0, 15), (0, edge - 2 * group)))
    b_own = jnp.concatenate([b_blocks.reshape(-1, edge), labels])

    a_line = lax.all_gather(a_own, "x_hi", axis=0)
    n_y = lax.axis_size("y")
    a_half = lax.all_to_all(
        jnp.broadcast_to(a_line[None], (n_y,) + a_line.shape), "y", split_axis=0, concat_axis=0, tiled=True
    ).reshape(-1, edge, edge)
    partner = lax.ppermute(a_half, "core", [(0, 1), (1, 0)])

    b_pieces = around(lax.all_gather(b_own, "x_lo", axis=0), "z")
    base = (group * lax.axis_index(COL) + lax.axis_index(ROW)) % panels
    place = jnp.stack([base, lax.axis_index("z"), lax.axis_index("core")]).astype(jnp.int32)
    outgoing = block_products(place, owner[0, 0], a_half, partner, b_pieces)
    arrived = lax.all_to_all(outgoing, COL, split_axis=0, concat_axis=0, tiled=True)
    return jnp.swapaxes(arrived, 0, 1)[:, None, None]


def solution(mesh):
    rows, columns = mesh.devices.shape
    fine = Mesh(
        mesh.devices.reshape(rows // (X_HI * CORES), X_HI, CORES, columns // X_LO, X_LO), ROW + COL
    )
    in_specs = (
        P(COL, ROW, None, None),
        P(COL, ROW),
        P(None, ROW, COL, None, None),
        P(None, ROW, COL),
        P(COL, ROW, None),
    )
    out_specs = P(None, COL, ROW, None, None, None)
    return jax.shard_map(shards, mesh=fine, in_specs=in_specs, out_specs=out_specs, check_vma=False)
```

time: 1030 us -> 135 us (0.13)
  the two profiles are of different devices: /device:TPU:64 before, /device:TPU:14 now
where the time goes in v1:
time: 135 us; the launch traced here: 132 us
  blocking collectives  53.4 us (40%)
  starting transfers between devices  46.3 us (34%)
  waiting for transfers between devices  20.5 us (15%)
  local copies, waits for them, and re-layouts  5.65 us (4%)
  Pallas kernels  4.87 us (4%)
    all_to_all x1, blocking collectives, shards(): lax.all_to_all(outgoing, COL, split_axis=0, concat_axis=0, tiled=True)  28.2 us
    ppermute x3, starting transfers between devices, around(): found[n - t] = lax.ppermute(found[(n - t + 1) % n], axis, down)  23.5 us
    all_gather x1, blocking collectives, shards(): a_line = lax.all_gather(a_own, 'x_hi', axis=0)  13.8 us
    ppermute x3, waiting for transfers between devices, around(): found[n - t] = lax.ppermute(found[(n - t + 1) % n], axis, down)  12.3 us
    all_gather x1, blocking collectives, shards(): b_pieces = around(lax.all_gather(b_own, 'x_lo', axis=0), 'z')  11.4 us
    all_to_all x1, starting transfers between devices, shards(): lax.all_to_all(jnp.broadcast_to(a_line[None], (n_y,) + a_line.shape), 'y'...  7.68 us
    ppermute x1, waiting for transfers between devices, around(): lax.ppermute(found[far - 1][0], axis, up)  6.33 us
    ppermute x3, starting transfers between devices, around(): found[t] = lax.ppermute(found[t - 1], axis, up)  5.75 us
  transfers between devices with their start and end apart: 10, of which 6 were waited for; matrix products, arithmetic and copies ran while one was open for 1% of the time, Pallas kernels for 0%

profile of v1, /device:TPU:14, one launch (start us, length us, event | category | flops | bytes accessed | tf_op | source)
XLA Modules:
  0.0 132.3 jit_solution(7525985091719229410)
XLA Ops:
  0.7 0.8 broadcast_select_fusion
  1.4 13.8 %all-gather = bf16[4,1,128,128]{3,2,1,0:T(8,128)(2,1)S(1)} all-gather(bf16[1,1,128,128]{3,2,1,0:T(8,128)(2,1)S(1)} %broadcast_select_fusion), channel_id=2, replica_groups=mesh['y'=8,'x_hi'=4,'core'=2,'z'=8,'x_lo'=2] {'x_hi'}, dimensions={0}, use_global_device_ids=true | all-gather | bytes 163840 | tf_op jit(solution)/shard_map/all_gather | solution.py:92
  15.2 1.2 broadcast_in_dim.13
  16.4 7.7 %all-to-all-start = ((bf16[8,4,128,128]{3,2,1,0:T(8,128)(2,1)}), bf16[8,4,128,128]{3,2,1,0:T(8,128)(2,1)S(1)}, u32[]{:S(2)}, u32[]{:S(2)}) async-start(bf16[8,4,128,128]{3,2,1,0:T(8,128)(2,1)} %broadcast_in_dim.13), calls=%async_computation | async-start | bytes 2097152 | tf_op jit(solution)/shard_map/all_to_all | solution.py:94
  24.1 0.1 convert_element_type.17
  24.2 11.4 %all-gather.1 = bf16[2080,128]{1,0:T(8,128)(2,1)S(1)} all-gather(bf16[1040,128]{1,0:T(8,128)(2,1)S(1)} %fusion.1), channel_id=3, replica_groups=mesh['y'=8,'x_hi'=4,'core'=2,'z'=8,'x_lo'=2] {'x_lo'}, dimensions={0}, use_global_device_ids=true | all-gather | bytes 798720 | tf_op jit(solution)/shard_map/all_gather | solution.py:99
  35.7 12.2 %collective-permute-start.5 = (bf16[2,1040,128]{2,1,0:T(8,128)(2,1)S(1)}, bf16[2,1040,128]{2,1,0:T(8,128)(2,1)S(1)}, u32[]{:S(2)}, u32[]{:S(2)}) collective-permute-start(bf16[2,1040,128]{2,1,0:T(8,128)(2,1)S(1)} %bitcast.18), channel_id=1, source_target_pairs={{0,14},{2,0},{4,2},{6,4},{8,6},{10,8},{12,10},{14,12},{1,15},{3,1}... | collective-permute-start | bytes 1597448 | tf_op jit(solution)/shard_map/ppermute | solution.py:75
  47.9 1.9 %collective-permute-start.1 = (bf16[2,1040,128]{2,1,0:T(8,128)(2,1)S(1)}, bf16[2,1040,128]{2,1,0:T(8,128)(2,1)S(1)}, u32[]{:S(2)}, u32[]{:S(2)}) collective-permute-start(bf16[2,1040,128]{2,1,0:T(8,128)(2,1)S(1)} %bitcast.19), channel_id=1, source_target_pairs={{0,2},{2,4},{4,6},{6,8},{8,10},{10,12},{12,14},{14,0},{1,3},{3,5},... | collective-permute-start | bytes 1597448 | tf_op jit(solution)/shard_map/ppermute | solution.py:74
  49.8 5.2 %collective-permute-done.5.refs_8_ = bf16[2,1040,128]{2,1,0:T(8,128)(2,1)S(1)} collective-permute-done((bf16[2,1040,128]{2,1,0:T(8,128)(2,1)S(1)}, bf16[2,1040,128]{2,1,0:T(8,128)(2,1)S(1)}, u32[]{:S(2)}, u32[]{:S(2)}) %collective-permute-start.5) | collective-permute-done | bytes 532512 | tf_op jit(solution)/shard_map/ppermute | solution.py:75
  55.0 5.6 %collective-permute-start.6 = (bf16[2,1040,128]{2,1,0:T(8,128)(2,1)S(1)}, bf16[2,1040,128]{2,1,0:T(8,128)(2,1)}, u32[]{:S(2)}, u32[]{:S(2)}) collective-permute-start(bf16[2,1040,128]{2,1,0:T(8,128)(2,1)S(1)} %collective-permute-done.5.refs_8_), channel_id=1, source_target_pairs={{0,14},{2,0},{4,2},{6,4},{8,6},{10,8},{12,10},{14,12},{1,15},{3,1}... | collective-permute-start | bytes 1597448 | tf_op jit(solution)/shard_map/ppermute | solution.py:75
  60.6 0.0 collective-permute-done.1.refs_1_
  60.6 1.9 %collective-permute-start.2 = (bf16[2,1040,128]{2,1,0:T(8,128)(2,1)S(1)}, bf16[2,1040,128]{2,1,0:T(8,128)(2,1)}, u32[]{:S(2)}, u32[]{:S(2)}) collective-permute-start(bf16[2,1040,128]{2,1,0:T(8,128)(2,1)S(1)} %collective-permute-done.1.refs_1_), channel_id=1, source_target_pairs={{0,2},{2,4},{4,6},{6,8},{8,10},{10,12},{12,14},{14,0},{1,3},{3,5},... | collective-permute-start | bytes 1597448 | tf_op jit(solution)/shard_map/ppermute | solution.py:74
  62.6 0.8 copy-done
  63.4 4.2 %collective-permute-done.6.refs_7_ = bf16[2,1040,128]{2,1,0:T(8,128)(2,1)} collective-permute-done((bf16[2,1040,128]{2,1,0:T(8,128)(2,1)S(1)}, bf16[2,1040,128]{2,1,0:T(8,128)(2,1)}, u32[]{:S(2)}, u32[]{:S(2)}) %collective-permute-start.6) | collective-permute-done | bytes 532512 | tf_op jit(solution)/shard_map/ppermute | solution.py:75
  67.6 5.7 %collective-permute-start.7 = (bf16[2,1040,128]{2,1,0:T(8,128)(2,1)}, bf16[2,1040,128]{2,1,0:T(8,128)(2,1)S(1)}, u32[]{:S(2)}, u32[]{:S(2)}) collective-permute-start(bf16[2,1040,128]{2,1,0:T(8,128)(2,1)} %collective-permute-done.6.refs_7_), channel_id=1, source_target_pairs={{0,14},{2,0},{4,2},{6,4},{8,6},{10,8},{12,10},{14,12},{1,15},{3,1}... | collective-permute-start | bytes 1597448 | tf_op jit(solution)/shard_map/ppermute | solution.py:75
  73.3 0.3 collective-permute-done.2.refs_2_
  73.7 1.9 %collective-permute-start.3 = (bf16[2,1040,128]{2,1,0:T(8,128)(2,1)}, bf16[2,1040,128]{2,1,0:T(8,128)(2,1)S(1)}, u32[]{:S(2)}, u32[]{:S(2)}) collective-permute-start(bf16[2,1040,128]{2,1,0:T(8,128)(2,1)} %collective-permute-done.2.refs_2_), channel_id=1, source_target_pairs={{0,2},{2,4},{4,6},{6,8},{8,10},{10,12},{12,14},{14,0},{1,3},{3,5},... | collective-permute-start | bytes 1597448 | tf_op jit(solution)/shard_map/ppermute | solution.py:74
  75.6 0.0 all-to-all-done
  75.6 1.9 %collective-permute-start = (bf16[32,128,128]{2,1,0:T(8,128)(2,1)S(1)}, bf16[32,128,128]{2,1,0:T(8,128)(2,1)}, u32[]{:S(2)}, u32[]{:S(2)}) collective-permute-start(bf16[32,128,128]{2,1,0:T(8,128)(2,1)S(1)} %bitcast.16), channel_id=1, source_target_pairs={{0,16},{16,0},{1,17},{17,1},{2,18},{18,2},{3,19},{19,3},{4,20},{20... | collective-permute-start | bytes 3145736 | tf_op jit(solution)/shard_map/ppermute | solution.py:97
  77.5 2.9 %collective-permute-done.7.refs_6_ = bf16[2,1040,128]{2,1,0:T(8,128)(2,1)S(1)} collective-permute-done((bf16[2,1040,128]{2,1,0:T(8,128)(2,1)}, bf16[2,1040,128]{2,1,0:T(8,128)(2,1)S(1)}, u32[]{:S(2)}, u32[]{:S(2)}) %collective-permute-start.7) | collective-permute-done | bytes 532512 | tf_op jit(solution)/shard_map/ppermute | solution.py:75
  80.4 0.7 slice_bitcast_fusion
  81.1 5.5 %collective-permute-start.8 = (bf16[1040,128]{1,0:T(8,128)(2,1)}, bf16[1040,128]{1,0:T(8,128)(2,1)S(1)}, u32[]{:S(2)}, u32[]{:S(2)}) collective-permute-start(bf16[1040,128]{1,0:T(8,128)(2,1)} %slice_bitcast_fusion), channel_id=1, source_target_pairs={{0,14},{2,0},{4,2},{6,4},{8,6},{10,8},{12,10},{14,12},{1,15},{3,1}... | collective-permute-start | bytes 798728 | tf_op jit(solution)/shard_map/ppermute | solution.py:79
  86.6 0.0 collective-permute-done.3.refs_3_
  86.6 0.7 slice_bitcast_fusion.1
  87.4 1.9 %collective-permute-start.4 = (bf16[1040,128]{1,0:T(8,128)(2,1)}, bf16[1040,128]{1,0:T(8,128)(2,1)}, u32[]{:S(2)}, u32[]{:S(2)}) collective-permute-start(bf16[1040,128]{1,0:T(8,128)(2,1)} %slice_bitcast_fusion.1), channel_id=1, source_target_pairs={{0,2},{2,4},{4,6},{6,8},{8,10},{10,12},{12,14},{14,0},{1,3},{3,5},... | collective-permute-start | bytes 798728 | tf_op jit(solution)/shard_map/ppermute | solution.py:78
  89.3 0.1 pad_add_fusion.place_ref
  89.4 1.5 %collective-permute-done.8.refs_5_ = bf16[1040,128]{1,0:T(8,128)(2,1)S(1)} collective-permute-done((bf16[1040,128]{1,0:T(8,128)(2,1)}, bf16[1040,128]{1,0:T(8,128)(2,1)S(1)}, u32[]{:S(2)}, u32[]{:S(2)}) %collective-permute-start.8) | collective-permute-done | bytes 266272 | tf_op jit(solution)/shard_map/ppermute | solution.py:79
  90.9 6.3 %collective-permute-done.4.refs_4_ = bf16[1040,128]{1,0:T(8,128)(2,1)} collective-permute-done((bf16[1040,128]{1,0:T(8,128)(2,1)}, bf16[1040,128]{1,0:T(8,128)(2,1)}, u32[]{:S(2)}, u32[]{:S(2)}) %collective-permute-start.4) | collective-permute-done | bytes 266272 | tf_op jit(solution)/shard_map/ppermute | solution.py:78
  97.2 1.0 copy-done.1
  98.2 4.9 %shard_map.55 = bf16[16,2,128,128]{3,2,1,0:T(8,128)(2,1)S(1)} custom-call(s32[3]{0:T(128)S(1)} %pad_add_fusion.place_ref, s32[16]{0:T(128)S(1)} %bitcast.21, bf16[32,128,128]{2,1,0:T(8,128)(2,1)S(1)} %bitcast.17, bf16[32,128,128]{2,1,0:T(8,128)(2,1)} %collective-permute-done.partner_ref, bf16[2,1040,128]{2,1,0:T(8,128)(2,1)S(1)} %bitcast.20, ...), custom_call_target="tpu_custom_call" | custom-call | tf_op jit(solution)/shard_map/pallas_call | solution.py:53
  103.1 28.2 %all_to_all.10 = bf16[16,2,128,128]{3,2,1,0:T(8,128)(2,1)S(1)} all-to-all(bf16[16,2,128,128]{3,2,1,0:T(8,128)(2,1)S(1)} %shard_map.55), channel_id=1, replica_groups=mesh['y'=8,'x_hi'=4,'core'=2,'z'=8,'x_lo'=2] {'z','x_lo'}, dimensions={0} | all-to-all | bytes 2097152 | tf_op jit(solution)/shard_map/all_to_all | solution.py:103
  131.3 1.0 copy.7
  (11 shorter events, 0.1 us)
Async XLA Ops:
  16.4 7.7 %copy-start.4 = (s32[2,1,4]{2,1,0:T(1,128)S(1)}, s32[2,1,4]{2,1,0:T(1,128)}, u32[]{:S(2)}) copy-start(s32[2,1,4]{2,1,0:T(1,128)} %param.8) | copy-start | bytes 100
  16.4 7.8 %copy-start.3 = (bf16[2,1,4,128,128]{4,3,2,1,0:T(8,128)(2,1)S(1)}, bf16[2,1,4,128,128]{4,3,2,1,0:T(8,128)(2,1)}, u32[]{:S(2)}) copy-start(bf16[2,1,4,128,128]{4,3,2,1,0:T(8,128)(2,1)} %param.7) | copy-start | bytes 786436
  16.4 59.1 %all-to-all-start = ((bf16[8,4,128,128]{3,2,1,0:T(8,128)(2,1)}), bf16[8,4,128,128]{3,2,1,0:T(8,128)(2,1)S(1)}, u32[]{:S(2)}, u32[]{:S(2)}) async-start(bf16[8,4,128,128]{3,2,1,0:T(8,128)(2,1)} %broadcast_in_dim.13), calls=%async_computation | async-start | bytes 2097152 | tf_op jit(solution)/shard_map/all_to_all | solution.py:94
  35.7 19.4 %collective-permute-start.5 = (bf16[2,1040,128]{2,1,0:T(8,128)(2,1)S(1)}, bf16[2,1040,128]{2,1,0:T(8,128)(2,1)S(1)}, u32[]{:S(2)}, u32[]{:S(2)}) collective-permute-start(bf16[2,1040,128]{2,1,0:T(8,128)(2,1)S(1)} %bitcast.18), channel_id=1, source_target_pairs={{0,14},{2,0},{4,2},{6,4},{8,6},{10,8},{12,10},{14,12},{1,15},{3,1}... | collective-permute-start | bytes 1597448 | tf_op jit(solution)/shard_map/ppermute | solution.py:75
  47.9 12.7 %collective-permute-start.1 = (bf16[2,1040,128]{2,1,0:T(8,128)(2,1)S(1)}, bf16[2,1040,128]{2,1,0:T(8,128)(2,1)S(1)}, u32[]{:S(2)}, u32[]{:S(2)}) collective-permute-start(bf16[2,1040,128]{2,1,0:T(8,128)(2,1)S(1)} %bitcast.19), channel_id=1, source_target_pairs={{0,2},{2,4},{4,6},{6,8},{8,10},{10,12},{12,14},{14,0},{1,3},{3,5},... | collective-permute-start | bytes 1597448 | tf_op jit(solution)/shard_map/ppermute | solution.py:74
  55.0 12.6 %collective-permute-start.6 = (bf16[2,1040,128]{2,1,0:T(8,128)(2,1)S(1)}, bf16[2,1040,128]{2,1,0:T(8,128)(2,1)}, u32[]{:S(2)}, u32[]{:S(2)}) collective-permute-start(bf16[2,1040,128]{2,1,0:T(8,128)(2,1)S(1)} %collective-permute-done.5.refs_8_), channel_id=1, source_target_pairs={{0,14},{2,0},{4,2},{6,4},{8,6},{10,8},{12,10},{14,12},{1,15},{3,1}... | collective-permute-start | bytes 1597448 | tf_op jit(solution)/shard_map/ppermute | solution.py:75
  60.6 13.0 %collective-permute-start.2 = (bf16[2,1040,128]{2,1,0:T(8,128)(2,1)S(1)}, bf16[2,1040,128]{2,1,0:T(8,128)(2,1)}, u32[]{:S(2)}, u32[]{:S(2)}) collective-permute-start(bf16[2,1040,128]{2,1,0:T(8,128)(2,1)S(1)} %collective-permute-done.1.refs_1_), channel_id=1, source_target_pairs={{0,2},{2,4},{4,6},{6,8},{8,10},{10,12},{12,14},{14,0},{1,3},{3,5},... | collective-permute-start | bytes 1597448 | tf_op jit(solution)/shard_map/ppermute | solution.py:74
  62.6 0.8 copy-start
  67.6 12.8 %collective-permute-start.7 = (bf16[2,1040,128]{2,1,0:T(8,128)(2,1)}, bf16[2,1040,128]{2,1,0:T(8,128)(2,1)S(1)}, u32[]{:S(2)}, u32[]{:S(2)}) collective-permute-start(bf16[2,1040,128]{2,1,0:T(8,128)(2,1)} %collective-permute-done.6.refs_7_), channel_id=1, source_target_pairs={{0,14},{2,0},{4,2},{6,4},{8,6},{10,8},{12,10},{14,12},{1,15},{3,1}... | collective-permute-start | bytes 1597448 | tf_op jit(solution)/shard_map/ppermute | solution.py:75
  73.7 13.0 %collective-permute-start.3 = (bf16[2,1040,128]{2,1,0:T(8,128)(2,1)}, bf16[2,1040,128]{2,1,0:T(8,128)(2,1)S(1)}, u32[]{:S(2)}, u32[]{:S(2)}) collective-permute-start(bf16[2,1040,128]{2,1,0:T(8,128)(2,1)} %collective-permute-done.2.refs_2_), channel_id=1, source_target_pairs={{0,2},{2,4},{4,6},{6,8},{8,10},{10,12},{12,14},{14,0},{1,3},{3,5},... | collective-permute-start | bytes 1597448 | tf_op jit(solution)/shard_map/ppermute | solution.py:74
  75.6 21.6 %collective-permute-start = (bf16[32,128,128]{2,1,0:T(8,128)(2,1)S(1)}, bf16[32,128,128]{2,1,0:T(8,128)(2,1)}, u32[]{:S(2)}, u32[]{:S(2)}) collective-permute-start(bf16[32,128,128]{2,1,0:T(8,128)(2,1)S(1)} %bitcast.16), channel_id=1, source_target_pairs={{0,16},{16,0},{1,17},{17,1},{2,18},{18,2},{3,19},{19,3},{4,20},{20... | collective-permute-start | bytes 3145736 | tf_op jit(solution)/shard_map/ppermute | solution.py:97
  81.1 9.7 %collective-permute-start.8 = (bf16[1040,128]{1,0:T(8,128)(2,1)}, bf16[1040,128]{1,0:T(8,128)(2,1)S(1)}, u32[]{:S(2)}, u32[]{:S(2)}) collective-permute-start(bf16[1040,128]{1,0:T(8,128)(2,1)} %slice_bitcast_fusion), channel_id=1, source_target_pairs={{0,14},{2,0},{4,2},{6,4},{8,6},{10,8},{12,10},{14,12},{1,15},{3,1}... | collective-permute-start | bytes 798728 | tf_op jit(solution)/shard_map/ppermute | solution.py:79
  87.4 9.8 %collective-permute-start.4 = (bf16[1040,128]{1,0:T(8,128)(2,1)}, bf16[1040,128]{1,0:T(8,128)(2,1)}, u32[]{:S(2)}, u32[]{:S(2)}) collective-permute-start(bf16[1040,128]{1,0:T(8,128)(2,1)} %slice_bitcast_fusion.1), channel_id=1, source_target_pairs={{0,2},{2,4},{4,6},{6,8},{8,10},{10,12},{12,14},{14,0},{1,3},{3,5},... | collective-permute-start | bytes 798728 | tf_op jit(solution)/shard_map/ppermute | solution.py:78
  89.4 7.8 %copy-start.2 = (s32[1,1,16]{2,1,0:T(1,128)S(1)}, s32[1,1,16]{2,1,0:T(1,128)}, u32[]{:S(2)}) copy-start(s32[1,1,16]{2,1,0:T(1,128)} %param.9) | copy-start | bytes 196
  97.2 1.0 copy-start.1

commit v2 on v1

v2 whole, which is shorter than its diff:
```python
import functools

import jax
import jax.numpy as jnp
from jax import lax
from jax.experimental import pallas as pl
from jax.experimental.pallas import tpu as pltpu
from jax.sharding import Mesh
from jax.sharding import PartitionSpec as P

BR = 1
CORES = 2
X_LO = 2
X_HI = 4
ROW = ("y", "x_hi", "core")
COL = ("z", "x_lo")


def add_products(place_ref, owner_ref, own_ref, partner_ref, sides, total, label_rows, labels, arrived):
    cores, half = CORES, own_ref.shape[0]
    panels = cores * half
    edge = own_ref.shape[1]
    group = (sides[0][2].shape[0] // edge) // 2
    for n, (_, _, side_ref) in enumerate(sides):
        row = side_ref[pl.ds(2 * group * edge, 16), :].astype(jnp.float32)[:8]
        label_rows[pl.ds(8 * n, 8), :] = row.astype(jnp.int32)
    copy = pltpu.make_async_copy(label_rows, labels, arrived)
    copy.start()
    total[...] = jnp.zeros_like(total)
    copy.wait()
    base, here, core = place_ref[0], place_ref[1], place_ref[2]
    planes = panels // (group * X_LO)

    for n, (away, low, side_ref) in enumerate(sides):
        plane = lax.rem(here + planes - away, planes)
        for j in range(group):
            m = (plane * X_LO + low) * group + j
            q = lax.rem(base + panels - m, panels)
            mine = lax.rem(q, cores) == core
            a = jnp.where(mine, own_ref[q // cores], partner_ref[q // cores])
            for o in range(2):
                target = owner_ref[labels[8 * n, o * group + j]]
                b = side_ref[pl.ds((o * group + j) * edge, edge), :]
                total[target, o] += jnp.dot(a, b, preferred_element_type=jnp.float32)


def near_products(aways, place_ref, owner_ref, own_ref, partner_ref, *refs):
    b_refs, (out_ref, *scratch) = refs[: len(aways)], refs[len(aways) :]
    sides = [(away, low, ref.at[low]) for away, ref in zip(aways, b_refs) for low in range(X_LO)]
    add_products(place_ref, owner_ref, own_ref, partner_ref, sides, out_ref, *scratch)


def far_products(away, place_ref, owner_ref, own_ref, partner_ref, near_ref, *refs):
    b_refs, (out_ref, total, *scratch) = refs[:X_LO], refs[X_LO:]
    sides = [(away, low, ref) for low, ref in enumerate(b_refs)]
    add_products(place_ref, owner_ref, own_ref, partner_ref, sides, total, *scratch)
    out_ref[...] = (near_ref[...] + total[...]).astype(out_ref.dtype)


def block_products(place, owner, a_own, a_partner, b_pieces):
    slots, edge = owner.shape[0], a_own.shape[-1]
    smem = pl.BlockSpec(memory_space=pltpu.SMEM)
    vmem = pl.BlockSpec(memory_space=pltpu.VMEM)
    far = len(b_pieces) // 2
    aways = [t for t in range(len(b_pieces)) if t != far]
    shape = (slots, 2, edge, edge)

    def scratch(sides):
        return [
            pltpu.VMEM((8 * sides, edge), jnp.int32),
            pltpu.SMEM((8 * sides, edge), jnp.int32),
            pltpu.SemaphoreType.DMA,
        ]

    def cost(sides):
        products = 2 * sides * (b_pieces[0].shape[1] // edge // 2)
        return pl.CostEstimate(flops=8 * products * edge**3, bytes_accessed=2**20, transcendentals=0)

    common = (place, owner, a_own, a_partner)
    near = pl.pallas_call(
        functools.partial(near_products, aways),
        out_shape=jax.ShapeDtypeStruct(shape, jnp.float32),
        in_specs=[smem, smem, vmem, vmem] + [vmem] * len(aways),
        out_specs=vmem,
        scratch_shapes=scratch(X_LO * len(aways)),
        compiler_params=pltpu.CompilerParams(vmem_limit_bytes=6 * 1024 * 1024),
        cost_estimate=cost(X_LO * len(aways)),
    )(*common, *[b_pieces[t] for t in aways])
    return pl.pallas_call(
        functools.partial(far_products, far),
        out_shape=jax.ShapeDtypeStruct(shape, jnp.bfloat16),
        in_specs=[smem, smem, vmem, vmem, vmem] + [vmem] * X_LO,
        out_specs=vmem,
        scratch_shapes=[pltpu.VMEM(shape, jnp.float32)] + scratch(X_LO),
        compiler_params=pltpu.CompilerParams(vmem_limit_bytes=6 * 1024 * 1024),
        cost_estimate=cost(X_LO),
    )(*common, near, *b_pieces[far])


def around(piece, axis):
    n = lax.axis_size(axis)
    up = [(i, (i + 1) % n) for i in range(n)]
    down = [(i, (i - 1) % n) for i in range(n)]
    found = [piece] + [None] * (n - 1)
    for t in range(1, (n - 1) // 2 + 1):
        found[t] = lax.ppermute(found[t - 1], axis, up)
        found[n - t] = lax.ppermute(found[(n - t + 1) % n], axis, down)
    far = n // 2
    found[far] = (
        lax.ppermute(found[far - 1][0], axis, up),
        lax.ppermute(found[(far + 1) % n][1], axis, down),
    )
    return found


def shards(a_blocks, a_rows, b_blocks, b_cols, owner):
    edge = a_blocks.shape[-1]
    panels = lax.axis_size(ROW)
    group = b_blocks.shape[2]
    a_own = jnp.where(a_rows[0, 0] < BR, a_blocks[0, 0], jnp.zeros_like(a_blocks[0, 0]))
    labels = jnp.pad(b_cols.reshape(1, -1).astype(jnp.bfloat16), ((0, 15), (0, edge - 2 * group)))
    b_own = jnp.concatenate([b_blocks.reshape(-1, edge), labels])

    b_other = lax.ppermute(b_own, "x_lo", [(0, 1), (1, 0)])
    low = lax.axis_index("x_lo")
    b_pair = jnp.where(low == 0, jnp.stack([b_own, b_other]), jnp.stack([b_other, b_own]))
    plane = ("y", "x_hi")
    a_half = lax.all_to_all(
        jnp.broadcast_to(a_own[None], (lax.axis_size(plane),) + a_own.shape), plane, split_axis=0, concat_axis=0, tiled=True
    )
    partner = lax.ppermute(a_half, "core", [(0, 1), (1, 0)])

    b_pieces = around(b_pair, "z")
    base = (group * lax.axis_index(COL) + lax.axis_index(ROW)) % panels
    place = jnp.stack([base, lax.axis_index("z"), lax.axis_index("core")]).astype(jnp.int32)
    outgoing = block_products(place, owner[0, 0], a_half, partner, b_pieces)
    arrived = lax.all_to_all(outgoing, COL, split_axis=0, concat_axis=0, tiled=True)
    return jnp.swapaxes(arrived, 0, 1)[:, None, None]


def solution(mesh):
    rows, columns = mesh.devices.shape
    fine = Mesh(
        mesh.devices.reshape(rows // (X_HI * CORES), X_HI, CORES, columns // X_LO, X_LO), ROW + COL
    )
    in_specs = (
        P(COL, ROW, None, None),
        P(COL, ROW),
        P(None, ROW, COL, None, None),
        P(None, ROW, COL),
        P(COL, ROW, None),
    )
    out_specs = P(None, COL, ROW, None, None, None)
    return jax.shard_map(shards, mesh=fine, in_specs=in_specs, out_specs=out_specs, check_vma=False)
```

time: 135 us -> 123 us (0.911); the launches traced: 132 us -> 122 us
  blocking collectives: 53.4 us -> 27.4 us
  starting transfers between devices: 46.3 us -> 58 us
  waiting for transfers between devices: 20.5 us -> 22.7 us
  other arithmetic: 0.89 us -> 2.64 us
  local copies, waits for them, and re-layouts: 5.65 us -> 4.24 us
    all_gather x2 -> x0, blocking collectives: 25.2 us -> none  [the longest x1 13.8 us: shards(): a_line = lax.all_gather(a_own, 'x_hi', axis=0)]
    ppermute x3, waiting for transfers between devices: 0.31 us -> 22.7 us  [around(): found[t] = lax.ppermute(found[t - 1], axis, up)]
    ppermute x3, waiting for transfers between devices: 12.3 us -> 0.01 us  [around(): found[n - t] = lax.ppermute(found[(n - t + 1) % n], axis, down)]
    all_to_all x1, starting transfers between devices: 7.68 us -> 16.8 us  [shards(): lax.all_to_all(jnp.broadcast_to(a_own[None], (lax.axis_size(plane),) + a_...]
    ppermute x1, waiting for transfers between devices: 6.33 us -> 0.01 us  [around(): lax.ppermute(found[far - 1][0], axis, up)]
    ppermute x0 -> x1, starting transfers between devices: none -> 3.34 us  [shards(): b_other = lax.ppermute(b_own, 'x_lo', [(0, 1), (1, 0)])]
    ppermute x1, waiting for transfers between devices: 1.48 us -> 0.01 us  [around(): lax.ppermute(found[(far + 1) % n][1], axis, down)]
    pallas_call x1 -> x2, Pallas kernels: 4.87 us -> 6.14 us  [the longest x1 4.18 us: block_products(): pl.pallas_call(functools.partial(near_products, aways), out_shape=jax.Sha...]
  transfers between devices with their start and end apart: 10 -> 11, of which waited for: 6 -> 3; matrix products, arithmetic and copies ran while one was open for 1% -> 2% of each run, Pallas kernels for 0% -> 3%
where the time goes in v2:
time: 123 us; the launch traced here: 122 us
  starting transfers between devices  58 us (47%)
  blocking collectives  27.4 us (22%)
  waiting for transfers between devices  22.7 us (18%)
  Pallas kernels  6.14 us (5%)
  local copies, waits for them, and re-layouts  4.24 us (3%)
  other arithmetic  2.64 us (2%)
    all_to_all x1, blocking collectives, shards(): lax.all_to_all(outgoing, COL, split_axis=0, concat_axis=0, tiled=True)  27.4 us
    ppermute x3, starting transfers between devices, around(): found[n - t] = lax.ppermute(found[(n - t + 1) % n], axis, down)  23.2 us
    ppermute x3, waiting for transfers between devices, around(): found[t] = lax.ppermute(found[t - 1], axis, up)  22.7 us
    all_to_all x1, starting transfers between devices, shards(): lax.all_to_all(jnp.broadcast_to(a_own[None], (lax.axis_size(plane),) + a_...  16.8 us
    ppermute x3, starting transfers between devices, around(): found[t] = lax.ppermute(found[t - 1], axis, up)  5.74 us
    ppermute x1, starting transfers between devices, around(): lax.ppermute(found[(far + 1) % n][1], axis, down)  5.13 us
    pallas_call x1, Pallas kernels, block_products(): pl.pallas_call(functools.partial(near_products, aways), out_shape=jax.Sha...  4.18 us
    ppermute x1, starting transfers between devices, shards(): b_other = lax.ppermute(b_own, 'x_lo', [(0, 1), (1, 0)])  3.34 us
  transfers between devices with their start and end apart: 11, of which 3 were waited for; matrix products, arithmetic and copies ran while one was open for 2% of the time, Pallas kernels for 3%

profile of v2, /device:TPU:14, one launch (start us, length us, event | category | flops | bytes accessed | tf_op | source)
XLA Modules:
  0.0 122.0 jit_solution(18057127556261006202)
XLA Ops:
  0.0 0.7 convert_reduce_fusion
  0.7 0.1 convert_element_type.17
  0.8 1.0 fusion.2
  1.8 3.3 %collective-permute-start.1 = (bf16[1040,128]{1,0:T(8,128)(2,1)S(1)}, bf16[1040,128]{1,0:T(8,128)(2,1)S(1)}, u32[]{:S(2)}, u32[]{:S(2)}) collective-permute-start(bf16[1040,128]{1,0:T(8,128)(2,1)S(1)} %get-tuple-element.6), channel_id=1, source_target_pairs={{0,1},{1,0},{2,3},{3,2},{4,5},{5,4},{6,7},{7,6},{8,9},{9,8},{10,11... | collective-permute-start | bytes 798728 | tf_op jit(solution)/shard_map/ppermute | solution.py:124
  5.8 0.8 select_bitcast_fusion
  6.6 1.2 broadcast_in_dim.13
  7.8 16.8 %all-to-all-start = ((bf16[32,128,128]{2,1,0:T(8,128)(2,1)}), bf16[32,128,128]{2,1,0:T(8,128)(2,1)S(1)}, u32[]{:S(2)}, u32[]{:S(2)}) async-start(bf16[32,128,128]{2,1,0:T(8,128)(2,1)} %broadcast_in_dim.13), calls=%async_computation | async-start | bytes 2097152 | tf_op jit(solution)/shard_map/all_to_all | solution.py:128
  24.6 0.0 collective-permute-done.1
  24.6 0.1 maximum_select_fusion.refs_0_
  24.7 1.9 %collective-permute-start.2 = (bf16[2,1040,128]{2,1,0:T(8,128)(2,1)S(1)}, bf16[2,1040,128]{2,1,0:T(8,128)(2,1)S(1)}, u32[]{:S(2)}, u32[]{:S(2)}) collective-permute-start(bf16[2,1040,128]{2,1,0:T(8,128)(2,1)S(1)} %maximum_select_fusion.refs_0_), channel_id=1, source_target_pairs={{0,2},{2,4},{4,6},{6,8},{8,10},{10,12},{12,14},{14,0},{1,3},{3,5},... | collective-permute-start | bytes 1597448 | tf_op jit(solution)/shard_map/ppermute | solution.py:106
  26.6 12.9 %collective-permute-start.5 = (bf16[2,1040,128]{2,1,0:T(8,128)(2,1)S(1)}, bf16[2,1040,128]{2,1,0:T(8,128)(2,1)S(1)}, u32[]{:S(2)}, u32[]{:S(2)}) collective-permute-start(bf16[2,1040,128]{2,1,0:T(8,128)(2,1)S(1)} %maximum_select_fusion.refs_0_), channel_id=1, source_target_pairs={{0,14},{2,0},{4,2},{6,4},{8,6},{10,8},{12,10},{14,12},{1,15},{3,1}... | collective-permute-start | bytes 1597448 | tf_op jit(solution)/shard_map/ppermute | solution.py:107
  39.6 9.3 %collective-permute-done.2.refs_1_ = bf16[2,1040,128]{2,1,0:T(8,128)(2,1)S(1)} collective-permute-done((bf16[2,1040,128]{2,1,0:T(8,128)(2,1)S(1)}, bf16[2,1040,128]{2,1,0:T(8,128)(2,1)S(1)}, u32[]{:S(2)}, u32[]{:S(2)}) %collective-permute-start.2) | collective-permute-done | bytes 532512 | tf_op jit(solution)/shard_map/ppermute | solution.py:106
  48.9 1.9 %collective-permute-start.3 = (bf16[2,1040,128]{2,1,0:T(8,128)(2,1)S(1)}, bf16[2,1040,128]{2,1,0:T(8,128)(2,1)}, u32[]{:S(2)}, u32[]{:S(2)}) collective-permute-start(bf16[2,1040,128]{2,1,0:T(8,128)(2,1)S(1)} %collective-permute-done.2.refs_1_), channel_id=1, source_target_pairs={{0,2},{2,4},{4,6},{6,8},{8,10},{10,12},{12,14},{14,0},{1,3},{3,5},... | collective-permute-start | bytes 1597448 | tf_op jit(solution)/shard_map/ppermute | solution.py:106
  50.8 0.0 collective-permute-done.5.refs_6_
  50.8 5.1 %collective-permute-start.6 = (bf16[2,1040,128]{2,1,0:T(8,128)(2,1)S(1)}, bf16[2,1040,128]{2,1,0:T(8,128)(2,1)}, u32[]{:S(2)}, u32[]{:S(2)}) collective-permute-start(bf16[2,1040,128]{2,1,0:T(8,128)(2,1)S(1)} %collective-permute-done.5.refs_6_), channel_id=1, source_target_pairs={{0,14},{2,0},{4,2},{6,4},{8,6},{10,8},{12,10},{14,12},{1,15},{3,1}... | collective-permute-start | bytes 1597448 | tf_op jit(solution)/shard_map/ppermute | solution.py:107
  55.9 0.8 copy-done
  56.8 7.7 %collective-permute-done.3.refs_2_ = bf16[2,1040,128]{2,1,0:T(8,128)(2,1)} collective-permute-done((bf16[2,1040,128]{2,1,0:T(8,128)(2,1)S(1)}, bf16[2,1040,128]{2,1,0:T(8,128)(2,1)}, u32[]{:S(2)}, u32[]{:S(2)}) %collective-permute-start.3) | collective-permute-done | bytes 532512 | tf_op jit(solution)/shard_map/ppermute | solution.py:106
  64.4 1.9 %collective-permute-start.4 = (bf16[2,1040,128]{2,1,0:T(8,128)(2,1)}, bf16[2,1040,128]{2,1,0:T(8,128)(2,1)S(1)}, u32[]{:S(2)}, u32[]{:S(2)}) collective-permute-start(bf16[2,1040,128]{2,1,0:T(8,128)(2,1)} %collective-permute-done.3.refs_2_), channel_id=1, source_target_pairs={{0,2},{2,4},{4,6},{6,8},{8,10},{10,12},{12,14},{14,0},{1,3},{3,5},... | collective-permute-start | bytes 1597448 | tf_op jit(solution)/shard_map/ppermute | solution.py:106
  66.3 0.0 collective-permute-done.6.refs_5_
  66.3 5.1 %collective-permute-start.7 = (bf16[2,1040,128]{2,1,0:T(8,128)(2,1)}, bf16[2,1040,128]{2,1,0:T(8,128)(2,1)S(1)}, u32[]{:S(2)}, u32[]{:S(2)}) collective-permute-start(bf16[2,1040,128]{2,1,0:T(8,128)(2,1)} %collective-permute-done.6.refs_5_), channel_id=1, source_target_pairs={{0,14},{2,0},{4,2},{6,4},{8,6},{10,8},{12,10},{14,12},{1,15},{3,1}... | collective-permute-start | bytes 1597448 | tf_op jit(solution)/shard_map/ppermute | solution.py:107
  71.5 1.9 %collective-permute-start = (bf16[32,128,128]{2,1,0:T(8,128)(2,1)S(1)}, bf16[32,128,128]{2,1,0:T(8,128)(2,1)S(1)}, u32[]{:S(2)}, u32[]{:S(2)}) collective-permute-start(bf16[32,128,128]{2,1,0:T(8,128)(2,1)S(1)} %all-to-all-done.own_ref), channel_id=1, source_target_pairs={{0,16},{16,0},{1,17},{17,1},{2,18},{18,2},{3,19},{19,3},{4,20},{20... | collective-permute-start | bytes 3145736 | tf_op jit(solution)/shard_map/ppermute | solution.py:131
  73.4 5.7 %collective-permute-done.4.refs_3_ = bf16[2,1040,128]{2,1,0:T(8,128)(2,1)S(1)} collective-permute-done((bf16[2,1040,128]{2,1,0:T(8,128)(2,1)}, bf16[2,1040,128]{2,1,0:T(8,128)(2,1)S(1)}, u32[]{:S(2)}, u32[]{:S(2)}) %collective-permute-start.4) | collective-permute-done | bytes 532512 | tf_op jit(solution)/shard_map/ppermute | solution.py:106
  79.2 1.9 %collective-permute-start.8 = (bf16[1040,128]{1,0:T(8,128)(2,1)S(1)}, bf16[1040,128]{1,0:T(8,128)(2,1)S(1)}, u32[]{:S(2)}, u32[]{:S(2)}) collective-permute-start(bf16[1040,128]{1,0:T(8,128)(2,1)S(1)} %slice_bitcast_fusion.1), channel_id=1, source_target_pairs={{0,2},{2,4},{4,6},{6,8},{8,10},{10,12},{12,14},{14,0},{1,3},{3,5},... | collective-permute-start | bytes 798728 | tf_op jit(solution)/shard_map/ppermute | solution.py:110
  81.1 0.0 collective-permute-done.7.refs_4_
  81.1 5.1 %collective-permute-start.9 = (bf16[1040,128]{1,0:T(8,128)(2,1)S(1)}, bf16[1040,128]{1,0:T(8,128)(2,1)S(1)}, u32[]{:S(2)}, u32[]{:S(2)}) collective-permute-start(bf16[1040,128]{1,0:T(8,128)(2,1)S(1)} %slice_bitcast_fusion), channel_id=1, source_target_pairs={{0,14},{2,0},{4,2},{6,4},{8,6},{10,8},{12,10},{14,12},{1,15},{3,1}... | collective-permute-start | bytes 798728 | tf_op jit(solution)/shard_map/ppermute | solution.py:111
  86.3 0.1 pad_add_fusion.place_ref
  86.4 0.0 collective-permute-done.partner_ref
  86.4 1.0 copy-done.1
  87.4 4.2 %shard_map.55.near_ref = f32[16,2,128,128]{3,2,1,0:T(8,128)S(1)} custom-call(s32[3]{0:T(128)S(1)} %pad_add_fusion.place_ref, s32[16]{0:T(128)S(1)} %bitcast.18, bf16[32,128,128]{2,1,0:T(8,128)(2,1)S(1)} %all-to-all-done.own_ref, bf16[32,128,128]{2,1,0:T(8,128)(2,1)S(1)} %collective-permute-done.partner_ref, ...), custom_call_target="tpu_custom_call" | custom-call | flops 1879048192 | bytes 1048576 | tf_op jit(solution)/shard_map/pallas_call | solution.py:80
  91.6 2.0 %shard_map.56 = bf16[16,2,128,128]{3,2,1,0:T(8,128)(2,1)S(1)} custom-call(s32[3]{0:T(128)S(1)} %pad_add_fusion.place_ref, s32[16]{0:T(128)S(1)} %bitcast.19, bf16[32,128,128]{2,1,0:T(8,128)(2,1)S(1)} %all-to-all-done.own_ref, bf16[32,128,128]{2,1,0:T(8,128)(2,1)S(1)} %collective-permute-done.partner_ref, f32[16,2,128,128]{3,2,1,0:T(8,128)S(1)} %shard_map.55.near_ref, ...), custom_call_target="tpu_custom_call" | custom-call | flops 268435456 | bytes 1048576 | tf_op jit(solution)/shard_map/pallas_call | solution.py:89
  93.6 27.4 %all_to_all.10 = bf16[16,2,128,128]{3,2,1,0:T(8,128)(2,1)S(1)} all-to-all(bf16[16,2,128,128]{3,2,1,0:T(8,128)(2,1)S(1)} %shard_map.56), channel_id=1, replica_groups=mesh['y'=8,'x_hi'=4,'core'=2,'z'=8,'x_lo'=2] {'z','x_lo'}, dimensions={0} | all-to-all | bytes 2097152 | tf_op jit(solution)/shard_map/all_to_all | solution.py:137
  121.0 1.0 copy.6
  (9 shorter events, 0.1 us)
Async XLA Ops:
  1.8 22.8 %collective-permute-start.1 = (bf16[1040,128]{1,0:T(8,128)(2,1)S(1)}, bf16[1040,128]{1,0:T(8,128)(2,1)S(1)}, u32[]{:S(2)}, u32[]{:S(2)}) collective-permute-start(bf16[1040,128]{1,0:T(8,128)(2,1)S(1)} %get-tuple-element.6), channel_id=1, source_target_pairs={{0,1},{1,0},{2,3},{3,2},{4,5},{5,4},{6,7},{7,6},{8,9},{9,8},{10,11... | collective-permute-start | bytes 798728 | tf_op jit(solution)/shard_map/ppermute | solution.py:124
  7.8 78.6 %copy-start.2 = (s32[1,1,16]{2,1,0:T(1,128)S(1)}, s32[1,1,16]{2,1,0:T(1,128)}, u32[]{:S(2)}) copy-start(s32[1,1,16]{2,1,0:T(1,128)} %param.9) | copy-start | bytes 196
  7.8 63.7 %all-to-all-start = ((bf16[32,128,128]{2,1,0:T(8,128)(2,1)}), bf16[32,128,128]{2,1,0:T(8,128)(2,1)S(1)}, u32[]{:S(2)}, u32[]{:S(2)}) async-start(bf16[32,128,128]{2,1,0:T(8,128)(2,1)} %broadcast_in_dim.13), calls=%async_computation | async-start | bytes 2097152 | tf_op jit(solution)/shard_map/all_to_all | solution.py:128
  24.7 24.2 %collective-permute-start.2 = (bf16[2,1040,128]{2,1,0:T(8,128)(2,1)S(1)}, bf16[2,1040,128]{2,1,0:T(8,128)(2,1)S(1)}, u32[]{:S(2)}, u32[]{:S(2)}) collective-permute-start(bf16[2,1040,128]{2,1,0:T(8,128)(2,1)S(1)} %maximum_select_fusion.refs_0_), channel_id=1, source_target_pairs={{0,2},{2,4},{4,6},{6,8},{8,10},{10,12},{12,14},{14,0},{1,3},{3,5},... | collective-permute-start | bytes 1597448 | tf_op jit(solution)/shard_map/ppermute | solution.py:106
  26.6 24.2 %collective-permute-start.5 = (bf16[2,1040,128]{2,1,0:T(8,128)(2,1)S(1)}, bf16[2,1040,128]{2,1,0:T(8,128)(2,1)S(1)}, u32[]{:S(2)}, u32[]{:S(2)}) collective-permute-start(bf16[2,1040,128]{2,1,0:T(8,128)(2,1)S(1)} %maximum_select_fusion.refs_0_), channel_id=1, source_target_pairs={{0,14},{2,0},{4,2},{6,4},{8,6},{10,8},{12,10},{14,12},{1,15},{3,1}... | collective-permute-start | bytes 1597448 | tf_op jit(solution)/shard_map/ppermute | solution.py:107
  48.9 15.6 %collective-permute-start.3 = (bf16[2,1040,128]{2,1,0:T(8,128)(2,1)S(1)}, bf16[2,1040,128]{2,1,0:T(8,128)(2,1)}, u32[]{:S(2)}, u32[]{:S(2)}) collective-permute-start(bf16[2,1040,128]{2,1,0:T(8,128)(2,1)S(1)} %collective-permute-done.2.refs_1_), channel_id=1, source_target_pairs={{0,2},{2,4},{4,6},{6,8},{8,10},{10,12},{12,14},{14,0},{1,3},{3,5},... | collective-permute-start | bytes 1597448 | tf_op jit(solution)/shard_map/ppermute | solution.py:106
  50.8 15.5 %collective-permute-start.6 = (bf16[2,1040,128]{2,1,0:T(8,128)(2,1)S(1)}, bf16[2,1040,128]{2,1,0:T(8,128)(2,1)}, u32[]{:S(2)}, u32[]{:S(2)}) collective-permute-start(bf16[2,1040,128]{2,1,0:T(8,128)(2,1)S(1)} %collective-permute-done.5.refs_6_), channel_id=1, source_target_pairs={{0,14},{2,0},{4,2},{6,4},{8,6},{10,8},{12,10},{14,12},{1,15},{3,1}... | collective-permute-start | bytes 1597448 | tf_op jit(solution)/shard_map/ppermute | solution.py:107
  55.9 0.8 copy-start
  64.4 14.7 %collective-permute-start.4 = (bf16[2,1040,128]{2,1,0:T(8,128)(2,1)}, bf16[2,1040,128]{2,1,0:T(8,128)(2,1)S(1)}, u32[]{:S(2)}, u32[]{:S(2)}) collective-permute-start(bf16[2,1040,128]{2,1,0:T(8,128)(2,1)} %collective-permute-done.3.refs_2_), channel_id=1, source_target_pairs={{0,2},{2,4},{4,6},{6,8},{8,10},{10,12},{12,14},{14,0},{1,3},{3,5},... | collective-permute-start | bytes 1597448 | tf_op jit(solution)/shard_map/ppermute | solution.py:106
  66.3 14.8 %collective-permute-start.7 = (bf16[2,1040,128]{2,1,0:T(8,128)(2,1)}, bf16[2,1040,128]{2,1,0:T(8,128)(2,1)S(1)}, u32[]{:S(2)}, u32[]{:S(2)}) collective-permute-start(bf16[2,1040,128]{2,1,0:T(8,128)(2,1)} %collective-permute-done.6.refs_5_), channel_id=1, source_target_pairs={{0,14},{2,0},{4,2},{6,4},{8,6},{10,8},{12,10},{14,12},{1,15},{3,1}... | collective-permute-start | bytes 1597448 | tf_op jit(solution)/shard_map/ppermute | solution.py:107
  71.5 14.8 %collective-permute-start = (bf16[32,128,128]{2,1,0:T(8,128)(2,1)S(1)}, bf16[32,128,128]{2,1,0:T(8,128)(2,1)S(1)}, u32[]{:S(2)}, u32[]{:S(2)}) collective-permute-start(bf16[32,128,128]{2,1,0:T(8,128)(2,1)S(1)} %all-to-all-done.own_ref), channel_id=1, source_target_pairs={{0,16},{16,0},{1,17},{17,1},{2,18},{18,2},{3,19},{19,3},{4,20},{20... | collective-permute-start | bytes 3145736 | tf_op jit(solution)/shard_map/ppermute | solution.py:131
  79.2 12.4 %collective-permute-start.8 = (bf16[1040,128]{1,0:T(8,128)(2,1)S(1)}, bf16[1040,128]{1,0:T(8,128)(2,1)S(1)}, u32[]{:S(2)}, u32[]{:S(2)}) collective-permute-start(bf16[1040,128]{1,0:T(8,128)(2,1)S(1)} %slice_bitcast_fusion.1), channel_id=1, source_target_pairs={{0,2},{2,4},{4,6},{6,8},{8,10},{10,12},{12,14},{14,0},{1,3},{3,5},... | collective-permute-start | bytes 798728 | tf_op jit(solution)/shard_map/ppermute | solution.py:110
  81.1 10.5 %collective-permute-start.9 = (bf16[1040,128]{1,0:T(8,128)(2,1)S(1)}, bf16[1040,128]{1,0:T(8,128)(2,1)S(1)}, u32[]{:S(2)}, u32[]{:S(2)}) collective-permute-start(bf16[1040,128]{1,0:T(8,128)(2,1)S(1)} %slice_bitcast_fusion), channel_id=1, source_target_pairs={{0,14},{2,0},{4,2},{6,4},{8,6},{10,8},{12,10},{14,12},{1,15},{3,1}... | collective-permute-start | bytes 798728 | tf_op jit(solution)/shard_map/ppermute | solution.py:111
  86.4 1.0 copy-start.1

commit v3 on v2

--- a/solution.py
+++ b/solution.py
@@ -16,7 +16,7 @@
 COL = ("z", "x_lo")
 
 
-def add_products(place_ref, owner_ref, own_ref, partner_ref, sides, total, label_rows, labels, arrived):
+def add_products(place_ref, owner_ref, own_ref, partner_ref, sides, start_ref, total, label_rows, labels, arrived):
     cores, half = CORES, own_ref.shape[0]
     panels = cores * half
     edge = own_ref.shape[1]
@@ -26,7 +26,7 @@
         label_rows[pl.ds(8 * n, 8), :] = row.astype(jnp.int32)
     copy = pltpu.make_async_copy(label_rows, labels, arrived)
     copy.start()
-    total[...] = jnp.zeros_like(total)
+    total[...] = jnp.zeros_like(total) if start_ref is None else start_ref[...]
     copy.wait()
     base, here, core = place_ref[0], place_ref[1], place_ref[2]
     planes = panels // (group * X_LO)
@@ -37,7 +37,9 @@
             m = (plane * X_LO + low) * group + j
             q = lax.rem(base + panels - m, panels)
             mine = lax.rem(q, cores) == core
-            a = jnp.where(mine, own_ref[q // cores], partner_ref[q // cores])
+            chip = q // cores
+            at = lax.rem(chip, X_HI) * (half // X_HI) + chip // X_HI
+            a = jnp.where(mine, own_ref[at], partner_ref[at])
             for o in range(2):
                 target = owner_ref[labels[8 * n, o * group + j]]
                 b = side_ref[pl.ds((o * group + j) * edge, edge), :]
@@ -47,14 +49,14 @@
 def near_products(aways, place_ref, owner_ref, own_ref, partner_ref, *refs):
     b_refs, (out_ref, *scratch) = refs[: len(aways)], refs[len(aways) :]
     sides = [(away, low, ref.at[low]) for away, ref in zip(aways, b_refs) for low in range(X_LO)]
-    add_products(place_ref, owner_ref, own_ref, partner_ref, sides, out_ref, *scratch)
+    add_products(place_ref, owner_ref, own_ref, partner_ref, sides, None, out_ref, *scratch)
 
 
 def far_products(away, place_ref, owner_ref, own_ref, partner_ref, near_ref, *refs):
     b_refs, (out_ref, total, *scratch) = refs[:X_LO], refs[X_LO:]
     sides = [(away, low, ref) for low, ref in enumerate(b_refs)]
-    add_products(place_ref, owner_ref, own_ref, partner_ref, sides, total, *scratch)
-    out_ref[...] = (near_ref[...] + total[...]).astype(out_ref.dtype)
+    add_products(place_ref, owner_ref, own_ref, partner_ref, sides, near_ref, total, *scratch)
+    out_ref[...] = total[...].astype(out_ref.dtype)
 
 
 def block_products(place, owner, a_own, a_partner, b_pieces):
@@ -124,7 +126,7 @@
     b_other = lax.ppermute(b_own, "x_lo", [(0, 1), (1, 0)])
     low = lax.axis_index("x_lo")
     b_pair = jnp.where(low == 0, jnp.stack([b_own, b_other]), jnp.stack([b_other, b_own]))
-    plane = ("y", "x_hi")
+    plane = ("x_hi", "y")
     a_half = lax.all_to_all(
         jnp.broadcast_to(a_own[None], (lax.axis_size(plane),) + a_own.shape), plane, split_axis=0, concat_axis=0, tiled=True
     )

time: 123 us -> 123 us (level)
  transfers between devices with their start and end apart: 11 -> 11, of which waited for: 3 -> 3; matrix products, arithmetic and copies ran while one was open for 2% -> 2% of each run, Pallas kernels for 3% -> 4%
where the time goes in v3:
time: 123 us; the launch traced here: 122 us
  starting transfers between devices  58.1 us (47%)
  blocking collectives  27 us (22%)
  waiting for transfers between devices  22.7 us (18%)
  Pallas kernels  6.19 us (5%)
  local copies, waits for them, and re-layouts  4.24 us (3%)
  other arithmetic  2.64 us (2%)
    all_to_all x1, blocking collectives, shards(): lax.all_to_all(outgoing, COL, split_axis=0, concat_axis=0, tiled=True)  27 us
    ppermute x3, starting transfers between devices, around(): found[n - t] = lax.ppermute(found[(n - t + 1) % n], axis, down)  23.1 us
    ppermute x3, waiting for transfers between devices, around(): found[t] = lax.ppermute(found[t - 1], axis, up)  22.7 us
    all_to_all x1, starting transfers between devices, shards(): lax.all_to_all(jnp.broadcast_to(a_own[None], (lax.axis_size(plane),) + a_...  16.9 us
    ppermute x3, starting transfers between devices, around(): found[t] = lax.ppermute(found[t - 1], axis, up)  5.74 us
    ppermute x1, starting transfers between devices, around(): lax.ppermute(found[(far + 1) % n][1], axis, down)  5.13 us
    pallas_call x1, Pallas kernels, block_products(): pl.pallas_call(functools.partial(near_products, aways), out_shape=jax.Sha...  4.52 us
    ppermute x1, starting transfers between devices, shards(): b_other = lax.ppermute(b_own, 'x_lo', [(0, 1), (1, 0)])  3.34 us
  transfers between devices with their start and end apart: 11, of which 3 were waited for; matrix products, arithmetic and copies ran while one was open for 2% of the time, Pallas kernels for 4%

profile of v3, /device:TPU:14, one launch (start us, length us, event | category | flops | bytes accessed | tf_op | source)
XLA Modules:
  0.0 121.8 jit_solution(2332081862006268809)
XLA Ops:
  0.0 0.7 convert_reduce_fusion
  0.7 0.1 convert_element_type.17
  0.8 1.0 fusion.2
  1.8 3.3 %collective-permute-start.1 = (bf16[1040,128]{1,0:T(8,128)(2,1)S(1)}, bf16[1040,128]{1,0:T(8,128)(2,1)S(1)}, u32[]{:S(2)}, u32[]{:S(2)}) collective-permute-start(bf16[1040,128]{1,0:T(8,128)(2,1)S(1)} %get-tuple-element.6), channel_id=1, source_target_pairs={{0,1},{1,0},{2,3},{3,2},{4,5},{5,4},{6,7},{7,6},{8,9},{9,8},{10,11... | collective-permute-start | bytes 798728 | tf_op jit(solution)/shard_map/ppermute | solution.py:126
  5.8 0.8 select_bitcast_fusion
  6.6 1.2 broadcast_in_dim.13
  7.8 16.9 %all-to-all-start = ((bf16[32,128,128]{2,1,0:T(8,128)(2,1)}), bf16[32,128,128]{2,1,0:T(8,128)(2,1)S(1)}, u32[]{:S(2)}, u32[]{:S(2)}) async-start(bf16[32,128,128]{2,1,0:T(8,128)(2,1)} %broadcast_in_dim.13), calls=%async_computation | async-start | bytes 2097152 | tf_op jit(solution)/shard_map/all_to_all | solution.py:130
  24.7 0.0 collective-permute-done.1
  24.7 0.1 maximum_select_fusion.refs_0_
  24.8 1.9 %collective-permute-start.2 = (bf16[2,1040,128]{2,1,0:T(8,128)(2,1)S(1)}, bf16[2,1040,128]{2,1,0:T(8,128)(2,1)S(1)}, u32[]{:S(2)}, u32[]{:S(2)}) collective-permute-start(bf16[2,1040,128]{2,1,0:T(8,128)(2,1)S(1)} %maximum_select_fusion.refs_0_), channel_id=1, source_target_pairs={{0,2},{2,4},{4,6},{6,8},{8,10},{10,12},{12,14},{14,0},{1,3},{3,5},... | collective-permute-start | bytes 1597448 | tf_op jit(solution)/shard_map/ppermute | solution.py:108
  26.7 12.8 %collective-permute-start.5 = (bf16[2,1040,128]{2,1,0:T(8,128)(2,1)S(1)}, bf16[2,1040,128]{2,1,0:T(8,128)(2,1)S(1)}, u32[]{:S(2)}, u32[]{:S(2)}) collective-permute-start(bf16[2,1040,128]{2,1,0:T(8,128)(2,1)S(1)} %maximum_select_fusion.refs_0_), channel_id=1, source_target_pairs={{0,14},{2,0},{4,2},{6,4},{8,6},{10,8},{12,10},{14,12},{1,15},{3,1}... | collective-permute-start | bytes 1597448 | tf_op jit(solution)/shard_map/ppermute | solution.py:109
  39.6 9.3 %collective-permute-done.2.refs_1_ = bf16[2,1040,128]{2,1,0:T(8,128)(2,1)S(1)} collective-permute-done((bf16[2,1040,128]{2,1,0:T(8,128)(2,1)S(1)}, bf16[2,1040,128]{2,1,0:T(8,128)(2,1)S(1)}, u32[]{:S(2)}, u32[]{:S(2)}) %collective-permute-start.2) | collective-permute-done | bytes 532512 | tf_op jit(solution)/shard_map/ppermute | solution.py:108
  48.9 1.9 %collective-permute-start.3 = (bf16[2,1040,128]{2,1,0:T(8,128)(2,1)S(1)}, bf16[2,1040,128]{2,1,0:T(8,128)(2,1)}, u32[]{:S(2)}, u32[]{:S(2)}) collective-permute-start(bf16[2,1040,128]{2,1,0:T(8,128)(2,1)S(1)} %collective-permute-done.2.refs_1_), channel_id=1, source_target_pairs={{0,2},{2,4},{4,6},{6,8},{8,10},{10,12},{12,14},{14,0},{1,3},{3,5},... | collective-permute-start | bytes 1597448 | tf_op jit(solution)/shard_map/ppermute | solution.py:108
  50.8 5.1 %collective-permute-start.6 = (bf16[2,1040,128]{2,1,0:T(8,128)(2,1)S(1)}, bf16[2,1040,128]{2,1,0:T(8,128)(2,1)}, u32[]{:S(2)}, u32[]{:S(2)}) collective-permute-start(bf16[2,1040,128]{2,1,0:T(8,128)(2,1)S(1)} %collective-permute-done.5.refs_6_), channel_id=1, source_target_pairs={{0,14},{2,0},{4,2},{6,4},{8,6},{10,8},{12,10},{14,12},{1,15},{3,1}... | collective-permute-start | bytes 1597448 | tf_op jit(solution)/shard_map/ppermute | solution.py:109
  56.0 0.8 copy-done
  56.8 7.7 %collective-permute-done.3.refs_2_ = bf16[2,1040,128]{2,1,0:T(8,128)(2,1)} collective-permute-done((bf16[2,1040,128]{2,1,0:T(8,128)(2,1)S(1)}, bf16[2,1040,128]{2,1,0:T(8,128)(2,1)}, u32[]{:S(2)}, u32[]{:S(2)}) %collective-permute-start.3) | collective-permute-done | bytes 532512 | tf_op jit(solution)/shard_map/ppermute | solution.py:108
  64.5 1.9 %collective-permute-start.4 = (bf16[2,1040,128]{2,1,0:T(8,128)(2,1)}, bf16[2,1040,128]{2,1,0:T(8,128)(2,1)S(1)}, u32[]{:S(2)}, u32[]{:S(2)}) collective-permute-start(bf16[2,1040,128]{2,1,0:T(8,128)(2,1)} %collective-permute-done.3.refs_2_), channel_id=1, source_target_pairs={{0,2},{2,4},{4,6},{6,8},{8,10},{10,12},{12,14},{14,0},{1,3},{3,5},... | collective-permute-start | bytes 1597448 | tf_op jit(solution)/shard_map/ppermute | solution.py:108
  66.4 0.0 collective-permute-done.6.refs_5_
  66.4 5.1 %collective-permute-start.7 = (bf16[2,1040,128]{2,1,0:T(8,128)(2,1)}, bf16[2,1040,128]{2,1,0:T(8,128)(2,1)S(1)}, u32[]{:S(2)}, u32[]{:S(2)}) collective-permute-start(bf16[2,1040,128]{2,1,0:T(8,128)(2,1)} %collective-permute-done.6.refs_5_), channel_id=1, source_target_pairs={{0,14},{2,0},{4,2},{6,4},{8,6},{10,8},{12,10},{14,12},{1,15},{3,1}... | collective-permute-start | bytes 1597448 | tf_op jit(solution)/shard_map/ppermute | solution.py:109
  71.6 0.0 all-to-all-done.own_ref
  71.6 1.9 %collective-permute-start = (bf16[32,128,128]{2,1,0:T(8,128)(2,1)S(1)}, bf16[32,128,128]{2,1,0:T(8,128)(2,1)S(1)}, u32[]{:S(2)}, u32[]{:S(2)}) collective-permute-start(bf16[32,128,128]{2,1,0:T(8,128)(2,1)S(1)} %all-to-all-done.own_ref), channel_id=1, source_target_pairs={{0,16},{16,0},{1,17},{17,1},{2,18},{18,2},{3,19},{19,3},{4,20},{20... | collective-permute-start | bytes 3145736 | tf_op jit(solution)/shard_map/ppermute | solution.py:133
  73.5 5.7 %collective-permute-done.4.refs_3_ = bf16[2,1040,128]{2,1,0:T(8,128)(2,1)S(1)} collective-permute-done((bf16[2,1040,128]{2,1,0:T(8,128)(2,1)}, bf16[2,1040,128]{2,1,0:T(8,128)(2,1)S(1)}, u32[]{:S(2)}, u32[]{:S(2)}) %collective-permute-start.4) | collective-permute-done | bytes 532512 | tf_op jit(solution)/shard_map/ppermute | solution.py:108
  79.2 1.9 %collective-permute-start.8 = (bf16[1040,128]{1,0:T(8,128)(2,1)S(1)}, bf16[1040,128]{1,0:T(8,128)(2,1)S(1)}, u32[]{:S(2)}, u32[]{:S(2)}) collective-permute-start(bf16[1040,128]{1,0:T(8,128)(2,1)S(1)} %slice_bitcast_fusion.1), channel_id=1, source_target_pairs={{0,2},{2,4},{4,6},{6,8},{8,10},{10,12},{12,14},{14,0},{1,3},{3,5},... | collective-permute-start | bytes 798728 | tf_op jit(solution)/shard_map/ppermute | solution.py:112
  81.2 5.1 %collective-permute-start.9 = (bf16[1040,128]{1,0:T(8,128)(2,1)S(1)}, bf16[1040,128]{1,0:T(8,128)(2,1)S(1)}, u32[]{:S(2)}, u32[]{:S(2)}) collective-permute-start(bf16[1040,128]{1,0:T(8,128)(2,1)S(1)} %slice_bitcast_fusion), channel_id=1, source_target_pairs={{0,14},{2,0},{4,2},{6,4},{8,6},{10,8},{12,10},{14,12},{1,15},{3,1}... | collective-permute-start | bytes 798728 | tf_op jit(solution)/shard_map/ppermute | solution.py:113
  86.3 0.1 pad_add_fusion.place_ref
  86.4 0.0 collective-permute-done.partner_ref
  86.4 1.0 copy-done.1
  87.5 4.5 %shard_map.55.near_ref = f32[16,2,128,128]{3,2,1,0:T(8,128)S(1)} custom-call(s32[3]{0:T(128)S(1)} %pad_add_fusion.place_ref, s32[16]{0:T(128)S(1)} %bitcast.18, bf16[32,128,128]{2,1,0:T(8,128)(2,1)S(1)} %all-to-all-done.own_ref, bf16[32,128,128]{2,1,0:T(8,128)(2,1)S(1)} %collective-permute-done.partner_ref, ...), custom_call_target="tpu_custom_call" | custom-call | flops 1879048192 | bytes 1048576 | tf_op jit(solution)/shard_map/pallas_call | solution.py:82
  92.0 0.0 collective-permute-done.8.refs_0_
  92.0 1.7 %shard_map.56 = bf16[16,2,128,128]{3,2,1,0:T(8,128)(2,1)S(1)} custom-call(s32[3]{0:T(128)S(1)} %pad_add_fusion.place_ref, s32[16]{0:T(128)S(1)} %bitcast.19, bf16[32,128,128]{2,1,0:T(8,128)(2,1)S(1)} %all-to-all-done.own_ref, bf16[32,128,128]{2,1,0:T(8,128)(2,1)S(1)} %collective-permute-done.partner_ref, f32[16,2,128,128]{3,2,1,0:T(8,128)S(1)} %shard_map.55.near_ref, ...), custom_call_target="tpu_custom_call" | custom-call | flops 268435456 | bytes 1048576 | tf_op jit(solution)/shard_map/pallas_call | solution.py:91
  93.7 27.0 %all_to_all.10 = bf16[16,2,128,128]{3,2,1,0:T(8,128)(2,1)S(1)} all-to-all(bf16[16,2,128,128]{3,2,1,0:T(8,128)(2,1)S(1)} %shard_map.56), channel_id=1, replica_groups=mesh['y'=8,'x_hi'=4,'core'=2,'z'=8,'x_lo'=2] {'z','x_lo'}, dimensions={0} | all-to-all | bytes 2097152 | tf_op jit(solution)/shard_map/all_to_all | solution.py:139
  120.7 1.0 copy.6
  (9 shorter events, 0.1 us)
Async XLA Ops:
  1.8 22.9 %collective-permute-start.1 = (bf16[1040,128]{1,0:T(8,128)(2,1)S(1)}, bf16[1040,128]{1,0:T(8,128)(2,1)S(1)}, u32[]{:S(2)}, u32[]{:S(2)}) collective-permute-start(bf16[1040,128]{1,0:T(8,128)(2,1)S(1)} %get-tuple-element.6), channel_id=1, source_target_pairs={{0,1},{1,0},{2,3},{3,2},{4,5},{5,4},{6,7},{7,6},{8,9},{9,8},{10,11... | collective-permute-start | bytes 798728 | tf_op jit(solution)/shard_map/ppermute | solution.py:126
  7.8 78.6 %copy-start.2 = (s32[1,1,16]{2,1,0:T(1,128)S(1)}, s32[1,1,16]{2,1,0:T(1,128)}, u32[]{:S(2)}) copy-start(s32[1,1,16]{2,1,0:T(1,128)} %param.9) | copy-start | bytes 196
  7.8 63.8 %all-to-all-start = ((bf16[32,128,128]{2,1,0:T(8,128)(2,1)}), bf16[32,128,128]{2,1,0:T(8,128)(2,1)S(1)}, u32[]{:S(2)}, u32[]{:S(2)}) async-start(bf16[32,128,128]{2,1,0:T(8,128)(2,1)} %broadcast_in_dim.13), calls=%async_computation | async-start | bytes 2097152 | tf_op jit(solution)/shard_map/all_to_all | solution.py:130
  24.8 24.1 %collective-permute-start.2 = (bf16[2,1040,128]{2,1,0:T(8,128)(2,1)S(1)}, bf16[2,1040,128]{2,1,0:T(8,128)(2,1)S(1)}, u32[]{:S(2)}, u32[]{:S(2)}) collective-permute-start(bf16[2,1040,128]{2,1,0:T(8,128)(2,1)S(1)} %maximum_select_fusion.refs_0_), channel_id=1, source_target_pairs={{0,2},{2,4},{4,6},{6,8},{8,10},{10,12},{12,14},{14,0},{1,3},{3,5},... | collective-permute-start | bytes 1597448 | tf_op jit(solution)/shard_map/ppermute | solution.py:108
  26.7 24.1 %collective-permute-start.5 = (bf16[2,1040,128]{2,1,0:T(8,128)(2,1)S(1)}, bf16[2,1040,128]{2,1,0:T(8,128)(2,1)S(1)}, u32[]{:S(2)}, u32[]{:S(2)}) collective-permute-start(bf16[2,1040,128]{2,1,0:T(8,128)(2,1)S(1)} %maximum_select_fusion.refs_0_), channel_id=1, source_target_pairs={{0,14},{2,0},{4,2},{6,4},{8,6},{10,8},{12,10},{14,12},{1,15},{3,1}... | collective-permute-start | bytes 1597448 | tf_op jit(solution)/shard_map/ppermute | solution.py:109
  48.9 15.6 %collective-permute-start.3 = (bf16[2,1040,128]{2,1,0:T(8,128)(2,1)S(1)}, bf16[2,1040,128]{2,1,0:T(8,128)(2,1)}, u32[]{:S(2)}, u32[]{:S(2)}) collective-permute-start(bf16[2,1040,128]{2,1,0:T(8,128)(2,1)S(1)} %collective-permute-done.2.refs_1_), channel_id=1, source_target_pairs={{0,2},{2,4},{4,6},{6,8},{8,10},{10,12},{12,14},{14,0},{1,3},{3,5},... | collective-permute-start | bytes 1597448 | tf_op jit(solution)/shard_map/ppermute | solution.py:108
  50.8 15.5 %collective-permute-start.6 = (bf16[2,1040,128]{2,1,0:T(8,128)(2,1)S(1)}, bf16[2,1040,128]{2,1,0:T(8,128)(2,1)}, u32[]{:S(2)}, u32[]{:S(2)}) collective-permute-start(bf16[2,1040,128]{2,1,0:T(8,128)(2,1)S(1)} %collective-permute-done.5.refs_6_), channel_id=1, source_target_pairs={{0,14},{2,0},{4,2},{6,4},{8,6},{10,8},{12,10},{14,12},{1,15},{3,1}... | collective-permute-start | bytes 1597448 | tf_op jit(solution)/shard_map/ppermute | solution.py:109
  56.0 0.8 copy-start
  64.5 14.7 %collective-permute-start.4 = (bf16[2,1040,128]{2,1,0:T(8,128)(2,1)}, bf16[2,1040,128]{2,1,0:T(8,128)(2,1)S(1)}, u32[]{:S(2)}, u32[]{:S(2)}) collective-permute-start(bf16[2,1040,128]{2,1,0:T(8,128)(2,1)} %collective-permute-done.3.refs_2_), channel_id=1, source_target_pairs={{0,2},{2,4},{4,6},{6,8},{8,10},{10,12},{12,14},{14,0},{1,3},{3,5},... | collective-permute-start | bytes 1597448 | tf_op jit(solution)/shard_map/ppermute | solution.py:108
  66.4 14.8 %collective-permute-start.7 = (bf16[2,1040,128]{2,1,0:T(8,128)(2,1)}, bf16[2,1040,128]{2,1,0:T(8,128)(2,1)S(1)}, u32[]{:S(2)}, u32[]{:S(2)}) collective-permute-start(bf16[2,1040,128]{2,1,0:T(8,128)(2,1)} %collective-permute-done.6.refs_5_), channel_id=1, source_target_pairs={{0,14},{2,0},{4,2},{6,4},{8,6},{10,8},{12,10},{14,12},{1,15},{3,1}... | collective-permute-start | bytes 1597448 | tf_op jit(solution)/shard_map/ppermute | solution.py:109
  71.6 14.8 %collective-permute-start = (bf16[32,128,128]{2,1,0:T(8,128)(2,1)S(1)}, bf16[32,128,128]{2,1,0:T(8,128)(2,1)S(1)}, u32[]{:S(2)}, u32[]{:S(2)}) collective-permute-start(bf16[32,128,128]{2,1,0:T(8,128)(2,1)S(1)} %all-to-all-done.own_ref), channel_id=1, source_target_pairs={{0,16},{16,0},{1,17},{17,1},{2,18},{18,2},{3,19},{19,3},{4,20},{20... | collective-permute-start | bytes 3145736 | tf_op jit(solution)/shard_map/ppermute | solution.py:133
  79.2 12.8 %collective-permute-start.8 = (bf16[1040,128]{1,0:T(8,128)(2,1)S(1)}, bf16[1040,128]{1,0:T(8,128)(2,1)S(1)}, u32[]{:S(2)}, u32[]{:S(2)}) collective-permute-start(bf16[1040,128]{1,0:T(8,128)(2,1)S(1)} %slice_bitcast_fusion.1), channel_id=1, source_target_pairs={{0,2},{2,4},{4,6},{6,8},{8,10},{10,12},{12,14},{14,0},{1,3},{3,5},... | collective-permute-start | bytes 798728 | tf_op jit(solution)/shard_map/ppermute | solution.py:112
  81.2 10.8 %collective-permute-start.9 = (bf16[1040,128]{1,0:T(8,128)(2,1)S(1)}, bf16[1040,128]{1,0:T(8,128)(2,1)S(1)}, u32[]{:S(2)}, u32[]{:S(2)}) collective-permute-start(bf16[1040,128]{1,0:T(8,128)(2,1)S(1)} %slice_bitcast_fusion), channel_id=1, source_target_pairs={{0,14},{2,0},{4,2},{6,4},{8,6},{10,8},{12,10},{14,12},{1,15},{3,1}... | collective-permute-start | bytes 798728 | tf_op jit(solution)/shard_map/ppermute | solution.py:113
  86.4 1.0 copy-start.1

commit v4 on v3

--- a/solution.py
+++ b/solution.py
@@ -41,7 +41,8 @@
             at = lax.rem(chip, X_HI) * (half // X_HI) + chip // X_HI
             a = jnp.where(mine, own_ref[at], partner_ref[at])
             for o in range(2):
-                target = owner_ref[labels[8 * n, o * group + j]]
+                place = owner_ref[labels[8 * n, o * group + j]]
+                target = lax.rem(place, X_LO) * (total.shape[0] // X_LO) + place // X_LO
                 b = side_ref[pl.ds((o * group + j) * edge, edge), :]
                 total[target, o] += jnp.dot(a, b, preferred_element_type=jnp.float32)
 
@@ -136,8 +137,9 @@
     base = (group * lax.axis_index(COL) + lax.axis_index(ROW)) % panels
     place = jnp.stack([base, lax.axis_index("z"), lax.axis_index("core")]).astype(jnp.int32)
     outgoing = block_products(place, owner[0, 0], a_half, partner, b_pieces)
-    arrived = lax.all_to_all(outgoing, COL, split_axis=0, concat_axis=0, tiled=True)
-    return jnp.swapaxes(arrived, 0, 1)[:, None, None]
+    arrived = lax.all_to_all(outgoing, COL[::-1], split_axis=0, concat_axis=0, tiled=True)
+    arrived = arrived.reshape(X_LO, -1, 2, edge, edge).transpose(2, 1, 0, 3, 4)
+    return arrived.reshape(2, 1, 1, -1, edge, edge)
 
 
 def solution(mesh):

time: 123 us -> 123 us (level)
  transfers between devices with their start and end apart: 11 -> 11, of which waited for: 3 -> 3; matrix products, arithmetic and copies ran while one was open for 2% -> 1% of each run, Pallas kernels for 4% -> 4%
where the time goes in v4:
time: 123 us
  starting transfers between devices  58.8 us (48%)
  blocking collectives  27.3 us (22%)
  waiting for transfers between devices  22.7 us (18%)
  Pallas kernels  6.71 us (5%)
  local copies, waits for them, and re-layouts  4.24 us (3%)
  other arithmetic  1.89 us (2%)
    all_to_all x1, blocking collectives, shards(): lax.all_to_all(outgoing, COL[::-1], split_axis=0, concat_axis=0, tiled=True)  27.3 us
    ppermute x3, starting transfers between devices, around(): found[n - t] = lax.ppermute(found[(n - t + 1) % n], axis, down)  23.1 us
    ppermute x3, waiting for transfers between devices, around(): found[t] = lax.ppermute(found[t - 1], axis, up)  22.7 us
    all_to_all x1, starting transfers between devices, shards(): lax.all_to_all(jnp.broadcast_to(a_own[None], (lax.axis_size(plane),) + a_...  17.7 us
    ppermute x3, starting transfers between devices, around(): found[t] = lax.ppermute(found[t - 1], axis, up)  5.74 us
    ppermute x1, starting transfers between devices, around(): lax.ppermute(found[(far + 1) % n][1], axis, down)  5.13 us
    pallas_call x1, Pallas kernels, block_products(): pl.pallas_call(functools.partial(near_products, aways), out_shape=jax.Sha...  5 us
    ppermute x1, starting transfers between devices, shards(): b_other = lax.ppermute(b_own, 'x_lo', [(0, 1), (1, 0)])  3.34 us
  transfers between devices with their start and end apart: 11, of which 3 were waited for; matrix products, arithmetic and copies ran while one was open for 1% of the time, Pallas kernels for 4%

profile of v4, /device:TPU:14, one launch (start us, length us, event | category | flops | bytes accessed | tf_op | source)
XLA Modules:
  0.0 122.6 jit_solution(15697826208395758776)
XLA Ops:
  0.0 0.7 convert_reduce_fusion
  0.7 0.1 convert_element_type.17
  0.8 1.0 fusion.2
  1.8 3.3 %collective-permute-start.1 = (bf16[1040,128]{1,0:T(8,128)(2,1)S(1)}, bf16[1040,128]{1,0:T(8,128)(2,1)S(1)}, u32[]{:S(2)}, u32[]{:S(2)}) collective-permute-start(bf16[1040,128]{1,0:T(8,128)(2,1)S(1)} %get-tuple-element.6), channel_id=1, source_target_pairs={{0,1},{1,0},{2,3},{3,2},{4,5},{5,4},{6,7},{7,6},{8,9},{9,8},{10,11... | collective-permute-start | bytes 798728 | tf_op jit(solution)/shard_map/ppermute | solution.py:127
  5.8 1.2 broadcast_in_dim.10
  7.0 17.7 %all-to-all-start = ((bf16[32,128,128]{2,1,0:T(8,128)(2,1)}), bf16[32,128,128]{2,1,0:T(8,128)(2,1)S(1)}, u32[]{:S(2)}, u32[]{:S(2)}) async-start(bf16[32,128,128]{2,1,0:T(8,128)(2,1)} %broadcast_in_dim.10), calls=%async_computation | async-start | bytes 2097152 | tf_op jit(solution)/shard_map/all_to_all | solution.py:131
  24.7 0.0 collective-permute-done.1
  24.7 0.1 maximum_select_fusion.refs_0_
  24.8 1.9 %collective-permute-start.2 = (bf16[2,1040,128]{2,1,0:T(8,128)(2,1)S(1)}, bf16[2,1040,128]{2,1,0:T(8,128)(2,1)S(1)}, u32[]{:S(2)}, u32[]{:S(2)}) collective-permute-start(bf16[2,1040,128]{2,1,0:T(8,128)(2,1)S(1)} %maximum_select_fusion.refs_0_), channel_id=1, source_target_pairs={{0,2},{2,4},{4,6},{6,8},{8,10},{10,12},{12,14},{14,0},{1,3},{3,5},... | collective-permute-start | bytes 1597448 | tf_op jit(solution)/shard_map/ppermute | solution.py:109
  26.7 12.8 %collective-permute-start.5 = (bf16[2,1040,128]{2,1,0:T(8,128)(2,1)S(1)}, bf16[2,1040,128]{2,1,0:T(8,128)(2,1)S(1)}, u32[]{:S(2)}, u32[]{:S(2)}) collective-permute-start(bf16[2,1040,128]{2,1,0:T(8,128)(2,1)S(1)} %maximum_select_fusion.refs_0_), channel_id=1, source_target_pairs={{0,14},{2,0},{4,2},{6,4},{8,6},{10,8},{12,10},{14,12},{1,15},{3,1}... | collective-permute-start | bytes 1597448 | tf_op jit(solution)/shard_map/ppermute | solution.py:110
  39.6 9.3 %collective-permute-done.2.refs_1_ = bf16[2,1040,128]{2,1,0:T(8,128)(2,1)S(1)} collective-permute-done((bf16[2,1040,128]{2,1,0:T(8,128)(2,1)S(1)}, bf16[2,1040,128]{2,1,0:T(8,128)(2,1)S(1)}, u32[]{:S(2)}, u32[]{:S(2)}) %collective-permute-start.2) | collective-permute-done | bytes 532512 | tf_op jit(solution)/shard_map/ppermute | solution.py:109
  48.9 1.9 %collective-permute-start.3 = (bf16[2,1040,128]{2,1,0:T(8,128)(2,1)S(1)}, bf16[2,1040,128]{2,1,0:T(8,128)(2,1)}, u32[]{:S(2)}, u32[]{:S(2)}) collective-permute-start(bf16[2,1040,128]{2,1,0:T(8,128)(2,1)S(1)} %collective-permute-done.2.refs_1_), channel_id=1, source_target_pairs={{0,2},{2,4},{4,6},{6,8},{8,10},{10,12},{12,14},{14,0},{1,3},{3,5},... | collective-permute-start | bytes 1597448 | tf_op jit(solution)/shard_map/ppermute | solution.py:109
  50.8 0.0 collective-permute-done.5.refs_6_
  50.8 5.1 %collective-permute-start.6 = (bf16[2,1040,128]{2,1,0:T(8,128)(2,1)S(1)}, bf16[2,1040,128]{2,1,0:T(8,128)(2,1)}, u32[]{:S(2)}, u32[]{:S(2)}) collective-permute-start(bf16[2,1040,128]{2,1,0:T(8,128)(2,1)S(1)} %collective-permute-done.5.refs_6_), channel_id=1, source_target_pairs={{0,14},{2,0},{4,2},{6,4},{8,6},{10,8},{12,10},{14,12},{1,15},{3,1}... | collective-permute-start | bytes 1597448 | tf_op jit(solution)/shard_map/ppermute | solution.py:110
  56.0 0.8 copy-done
  56.8 7.7 %collective-permute-done.3.refs_2_ = bf16[2,1040,128]{2,1,0:T(8,128)(2,1)} collective-permute-done((bf16[2,1040,128]{2,1,0:T(8,128)(2,1)S(1)}, bf16[2,1040,128]{2,1,0:T(8,128)(2,1)}, u32[]{:S(2)}, u32[]{:S(2)}) %collective-permute-start.3) | collective-permute-done | bytes 532512 | tf_op jit(solution)/shard_map/ppermute | solution.py:109
  64.5 1.9 %collective-permute-start.4 = (bf16[2,1040,128]{2,1,0:T(8,128)(2,1)}, bf16[2,1040,128]{2,1,0:T(8,128)(2,1)S(1)}, u32[]{:S(2)}, u32[]{:S(2)}) collective-permute-start(bf16[2,1040,128]{2,1,0:T(8,128)(2,1)} %collective-permute-done.3.refs_2_), channel_id=1, source_target_pairs={{0,2},{2,4},{4,6},{6,8},{8,10},{10,12},{12,14},{14,0},{1,3},{3,5},... | collective-permute-start | bytes 1597448 | tf_op jit(solution)/shard_map/ppermute | solution.py:109
  66.4 0.0 collective-permute-done.6.refs_5_
  66.4 5.1 %collective-permute-start.7 = (bf16[2,1040,128]{2,1,0:T(8,128)(2,1)}, bf16[2,1040,128]{2,1,0:T(8,128)(2,1)S(1)}, u32[]{:S(2)}, u32[]{:S(2)}) collective-permute-start(bf16[2,1040,128]{2,1,0:T(8,128)(2,1)} %collective-permute-done.6.refs_5_), channel_id=1, source_target_pairs={{0,14},{2,0},{4,2},{6,4},{8,6},{10,8},{12,10},{14,12},{1,15},{3,1}... | collective-permute-start | bytes 1597448 | tf_op jit(solution)/shard_map/ppermute | solution.py:110
  71.6 1.9 %collective-permute-start = (bf16[32,128,128]{2,1,0:T(8,128)(2,1)S(1)}, bf16[32,128,128]{2,1,0:T(8,128)(2,1)S(1)}, u32[]{:S(2)}, u32[]{:S(2)}) collective-permute-start(bf16[32,128,128]{2,1,0:T(8,128)(2,1)S(1)} %all-to-all-done.own_ref), channel_id=1, source_target_pairs={{0,16},{16,0},{1,17},{17,1},{2,18},{18,2},{3,19},{19,3},{4,20},{20... | collective-permute-start | bytes 3145736 | tf_op jit(solution)/shard_map/ppermute | solution.py:134
  73.5 5.7 %collective-permute-done.4.refs_3_ = bf16[2,1040,128]{2,1,0:T(8,128)(2,1)S(1)} collective-permute-done((bf16[2,1040,128]{2,1,0:T(8,128)(2,1)}, bf16[2,1040,128]{2,1,0:T(8,128)(2,1)S(1)}, u32[]{:S(2)}, u32[]{:S(2)}) %collective-permute-start.4) | collective-permute-done | bytes 532512 | tf_op jit(solution)/shard_map/ppermute | solution.py:109
  79.2 1.9 %collective-permute-start.8 = (bf16[1040,128]{1,0:T(8,128)(2,1)S(1)}, bf16[1040,128]{1,0:T(8,128)(2,1)S(1)}, u32[]{:S(2)}, u32[]{:S(2)}) collective-permute-start(bf16[1040,128]{1,0:T(8,128)(2,1)S(1)} %slice_bitcast_fusion.1), channel_id=1, source_target_pairs={{0,2},{2,4},{4,6},{6,8},{8,10},{10,12},{12,14},{14,0},{1,3},{3,5},... | collective-permute-start | bytes 798728 | tf_op jit(solution)/shard_map/ppermute | solution.py:113
  81.2 0.0 collective-permute-done.7.refs_4_
  81.2 5.1 %collective-permute-start.9 = (bf16[1040,128]{1,0:T(8,128)(2,1)S(1)}, bf16[1040,128]{1,0:T(8,128)(2,1)S(1)}, u32[]{:S(2)}, u32[]{:S(2)}) collective-permute-start(bf16[1040,128]{1,0:T(8,128)(2,1)S(1)} %slice_bitcast_fusion), channel_id=1, source_target_pairs={{0,14},{2,0},{4,2},{6,4},{8,6},{10,8},{12,10},{14,12},{1,15},{3,1}... | collective-permute-start | bytes 798728 | tf_op jit(solution)/shard_map/ppermute | solution.py:114
  86.3 0.1 pad_add_fusion.place_ref
  86.4 0.0 collective-permute-done.partner_ref
  86.4 1.0 copy-done.1
  87.5 5.0 %shard_map.55.near_ref = f32[16,2,128,128]{3,2,1,0:T(8,128)S(1)} custom-call(s32[3]{0:T(128)S(1)} %pad_add_fusion.place_ref, s32[16]{0:T(128)S(1)} %bitcast.19, bf16[32,128,128]{2,1,0:T(8,128)(2,1)S(1)} %all-to-all-done.own_ref, bf16[32,128,128]{2,1,0:T(8,128)(2,1)S(1)} %collective-permute-done.partner_ref, ...), custom_call_target="tpu_custom_call" | custom-call | flops 1879048192 | bytes 1048576 | tf_op jit(solution)/shard_map/pallas_call | solution.py:83
  92.5 0.0 collective-permute-done.9.refs_1_
  92.5 1.7 %shard_map.56 = bf16[16,2,128,128]{3,2,1,0:T(8,128)(2,1)S(1)} custom-call(s32[3]{0:T(128)S(1)} %pad_add_fusion.place_ref, s32[16]{0:T(128)S(1)} %bitcast.20, bf16[32,128,128]{2,1,0:T(8,128)(2,1)S(1)} %all-to-all-done.own_ref, bf16[32,128,128]{2,1,0:T(8,128)(2,1)S(1)} %collective-permute-done.partner_ref, f32[16,2,128,128]{3,2,1,0:T(8,128)S(1)} %shard_map.55.near_ref, ...), custom_call_target="tpu_custom_call" | custom-call | flops 268435456 | bytes 1048576 | tf_op jit(solution)/shard_map/pallas_call | solution.py:92
  94.2 27.3 %all_to_all.10 = bf16[16,2,128,128]{3,2,1,0:T(8,128)(2,1)S(1)} all-to-all(bf16[16,2,128,128]{3,2,1,0:T(8,128)(2,1)S(1)} %shard_map.56), channel_id=1, replica_groups=mesh['y'=8,'x_hi'=4,'core'=2,'z'=8,'x_lo'=2] {'x_lo','z'}, dimensions={0} | all-to-all | bytes 2097152 | tf_op jit(solution)/shard_map/all_to_all | solution.py:140
  121.6 1.0 copy.6
  (9 shorter events, 0.1 us)
Async XLA Ops:
  1.8 22.9 %collective-permute-start.1 = (bf16[1040,128]{1,0:T(8,128)(2,1)S(1)}, bf16[1040,128]{1,0:T(8,128)(2,1)S(1)}, u32[]{:S(2)}, u32[]{:S(2)}) collective-permute-start(bf16[1040,128]{1,0:T(8,128)(2,1)S(1)} %get-tuple-element.6), channel_id=1, source_target_pairs={{0,1},{1,0},{2,3},{3,2},{4,5},{5,4},{6,7},{7,6},{8,9},{9,8},{10,11... | collective-permute-start | bytes 798728 | tf_op jit(solution)/shard_map/ppermute | solution.py:127
  7.0 79.4 %copy-start.2 = (s32[1,1,16]{2,1,0:T(1,128)S(1)}, s32[1,1,16]{2,1,0:T(1,128)}, u32[]{:S(2)}) copy-start(s32[1,1,16]{2,1,0:T(1,128)} %param.9) | copy-start | bytes 196
  7.0 64.5 %all-to-all-start = ((bf16[32,128,128]{2,1,0:T(8,128)(2,1)}), bf16[32,128,128]{2,1,0:T(8,128)(2,1)S(1)}, u32[]{:S(2)}, u32[]{:S(2)}) async-start(bf16[32,128,128]{2,1,0:T(8,128)(2,1)} %broadcast_in_dim.10), calls=%async_computation | async-start | bytes 2097152 | tf_op jit(solution)/shard_map/all_to_all | solution.py:131
  24.8 24.1 %collective-permute-start.2 = (bf16[2,1040,128]{2,1,0:T(8,128)(2,1)S(1)}, bf16[2,1040,128]{2,1,0:T(8,128)(2,1)S(1)}, u32[]{:S(2)}, u32[]{:S(2)}) collective-permute-start(bf16[2,1040,128]{2,1,0:T(8,128)(2,1)S(1)} %maximum_select_fusion.refs_0_), channel_id=1, source_target_pairs={{0,2},{2,4},{4,6},{6,8},{8,10},{10,12},{12,14},{14,0},{1,3},{3,5},... | collective-permute-start | bytes 1597448 | tf_op jit(solution)/shard_map/ppermute | solution.py:109
  26.7 24.1 %collective-permute-start.5 = (bf16[2,1040,128]{2,1,0:T(8,128)(2,1)S(1)}, bf16[2,1040,128]{2,1,0:T(8,128)(2,1)S(1)}, u32[]{:S(2)}, u32[]{:S(2)}) collective-permute-start(bf16[2,1040,128]{2,1,0:T(8,128)(2,1)S(1)} %maximum_select_fusion.refs_0_), channel_id=1, source_target_pairs={{0,14},{2,0},{4,2},{6,4},{8,6},{10,8},{12,10},{14,12},{1,15},{3,1}... | collective-permute-start | bytes 1597448 | tf_op jit(solution)/shard_map/ppermute | solution.py:110
  48.9 15.6 %collective-permute-start.3 = (bf16[2,1040,128]{2,1,0:T(8,128)(2,1)S(1)}, bf16[2,1040,128]{2,1,0:T(8,128)(2,1)}, u32[]{:S(2)}, u32[]{:S(2)}) collective-permute-start(bf16[2,1040,128]{2,1,0:T(8,128)(2,1)S(1)} %collective-permute-done.2.refs_1_), channel_id=1, source_target_pairs={{0,2},{2,4},{4,6},{6,8},{8,10},{10,12},{12,14},{14,0},{1,3},{3,5},... | collective-permute-start | bytes 1597448 | tf_op jit(solution)/shard_map/ppermute | solution.py:109
  50.8 15.5 %collective-permute-start.6 = (bf16[2,1040,128]{2,1,0:T(8,128)(2,1)S(1)}, bf16[2,1040,128]{2,1,0:T(8,128)(2,1)}, u32[]{:S(2)}, u32[]{:S(2)}) collective-permute-start(bf16[2,1040,128]{2,1,0:T(8,128)(2,1)S(1)} %collective-permute-done.5.refs_6_), channel_id=1, source_target_pairs={{0,14},{2,0},{4,2},{6,4},{8,6},{10,8},{12,10},{14,12},{1,15},{3,1}... | collective-permute-start | bytes 1597448 | tf_op jit(solution)/shard_map/ppermute | solution.py:110
  56.0 0.8 copy-start
  64.5 14.7 %collective-permute-start.4 = (bf16[2,1040,128]{2,1,0:T(8,128)(2,1)}, bf16[2,1040,128]{2,1,0:T(8,128)(2,1)S(1)}, u32[]{:S(2)}, u32[]{:S(2)}) collective-permute-start(bf16[2,1040,128]{2,1,0:T(8,128)(2,1)} %collective-permute-done.3.refs_2_), channel_id=1, source_target_pairs={{0,2},{2,4},{4,6},{6,8},{8,10},{10,12},{12,14},{14,0},{1,3},{3,5},... | collective-permute-start | bytes 1597448 | tf_op jit(solution)/shard_map/ppermute | solution.py:109
  66.4 14.8 %collective-permute-start.7 = (bf16[2,1040,128]{2,1,0:T(8,128)(2,1)}, bf16[2,1040,128]{2,1,0:T(8,128)(2,1)S(1)}, u32[]{:S(2)}, u32[]{:S(2)}) collective-permute-start(bf16[2,1040,128]{2,1,0:T(8,128)(2,1)} %collective-permute-done.6.refs_5_), channel_id=1, source_target_pairs={{0,14},{2,0},{4,2},{6,4},{8,6},{10,8},{12,10},{14,12},{1,15},{3,1}... | collective-permute-start | bytes 1597448 | tf_op jit(solution)/shard_map/ppermute | solution.py:110
  71.6 14.8 %collective-permute-start = (bf16[32,128,128]{2,1,0:T(8,128)(2,1)S(1)}, bf16[32,128,128]{2,1,0:T(8,128)(2,1)S(1)}, u32[]{:S(2)}, u32[]{:S(2)}) collective-permute-start(bf16[32,128,128]{2,1,0:T(8,128)(2,1)S(1)} %all-to-all-done.own_ref), channel_id=1, source_target_pairs={{0,16},{16,0},{1,17},{17,1},{2,18},{18,2},{3,19},{19,3},{4,20},{20... | collective-permute-start | bytes 3145736 | tf_op jit(solution)/shard_map/ppermute | solution.py:134
  79.2 13.3 %collective-permute-start.8 = (bf16[1040,128]{1,0:T(8,128)(2,1)S(1)}, bf16[1040,128]{1,0:T(8,128)(2,1)S(1)}, u32[]{:S(2)}, u32[]{:S(2)}) collective-permute-start(bf16[1040,128]{1,0:T(8,128)(2,1)S(1)} %slice_bitcast_fusion.1), channel_id=1, source_target_pairs={{0,2},{2,4},{4,6},{6,8},{8,10},{10,12},{12,14},{14,0},{1,3},{3,5},... | collective-permute-start | bytes 798728 | tf_op jit(solution)/shard_map/ppermute | solution.py:113
  81.2 11.3 %collective-permute-start.9 = (bf16[1040,128]{1,0:T(8,128)(2,1)S(1)}, bf16[1040,128]{1,0:T(8,128)(2,1)S(1)}, u32[]{:S(2)}, u32[]{:S(2)}) collective-permute-start(bf16[1040,128]{1,0:T(8,128)(2,1)S(1)} %slice_bitcast_fusion), channel_id=1, source_target_pairs={{0,14},{2,0},{4,2},{6,4},{8,6},{10,8},{12,10},{14,12},{1,15},{3,1}... | collective-permute-start | bytes 798728 | tf_op jit(solution)/shard_map/ppermute | solution.py:114
  86.4 1.0 copy-start.1
